TPU v7x, 32 devices: a whole 2x2x4 slice. The times are simulated.
32 devices in a mesh: gy: 8 (over z, core), gx: 4 (over y, x).
Axes of the slice: x: 2, y: 2, z: 4, core: 2. Of those that a mesh axis runs over, the one named last changes fastest.
Arguments:
- e_field: float32 [3, 4, 512, 512], P(None, None, 'gy', 'gx'), may hold values from -6 to 6
- h_field: float32 [3, 4, 512, 512], P(None, None, 'gy', 'gx'), may hold values from -6 to 6
- j_field: float32 [3, 4, 512, 512], P(None, None, 'gy', 'gx'), may hold values from -3 to 3
- material: int32 [4, 512, 512], P(None, 'gy', 'gx'), may hold values from 0 to 31
- material_table: float32 [4, 32], replicated, may hold values from 0.05 to 1
- dft_e: float32 [3, 2, 3, 4, 512, 512], P(None, None, None, None, 'gy', 'gx'), may hold values from -5 to 7
- dft_h: float32 [3, 2, 3, 4, 512, 512], P(None, None, None, None, 'gy', 'gx'), may hold values from -5 to 7
- skin_cell: int32 [32, 32, 128], P(('gy', 'gx')), may hold values from 0 to 32767, as said below
- counts: int32 [32, 32], P(('gy', 'gx')), may hold values from 0 to 128, as said below
- patch_slot: int32 [32, 32, 128], P(('gy', 'gx')), may hold values from 0 to 65535
- area: float32 [3, 2048, 1024], P(None, 'gy', 'gx'), may hold values from -0.5 to 1.5
Outputs:
- e_next: float32 [3, 4, 512, 512], P(None, None, 'gy', 'gx')
- j_next: float32 [3, 4, 512, 512], P(None, None, 'gy', 'gx')
- dft_e_next: float32 [3, 2, 3, 4, 512, 512], P(None, None, None, None, 'gy', 'gx')
- dft_h_next: float32 [3, 2, 3, 4, 512, 512], P(None, None, None, None, 'gy', 'gx')
- point_density: float32 [3, 2048, 1024], P(None, 'gy', 'gx')
- avg_density: float32 [3, 2048, 1024], P(None, 'gy', 'gx')
Inputs may be any that keep to these rules, and one draw needn't show every extreme that they name: Within one source block s the entries skin_cell[s, :, :] are distinct. Some owner block d has counts[s, d] = 128 for every source block s.
All inputs are finite; a program needn't handle non-finite values.
Results may differ from a plain program's by a relative error of at most 0.0003.
Values sent between devices are 32-bit elements; how exact they have to be, the bound alone decides.
A program may use at most 192 MiB of HBM per device.

v0:
```python
import math

import jax
import jax.numpy as jnp
from jax import lax
from jax.sharding import PartitionSpec as P

STEP = 1000
HALF = 100


FREQ_LIST = (28000000000.0, 39000000000.0, 60000000000.0)
TIME_STEP = 1.9e-13


def shifted(value, axis, steps):
    count = lax.axis_size(axis)
    leading, last = (max(0, -steps), min(count, count - steps))
    return lax.ppermute(value, axis, [(source, source + steps) for source in range(leading, last)])


def with_halo(cells, sides, width):
    for axis, dim in sides:
        count = lax.axis_size(axis)
        ends = count - 1
        head = lax.slice_in_dim(cells, 0, width, axis=dim)
        tail = lax.slice_in_dim(cells, cells.shape[dim] - width, cells.shape[dim], axis=dim)
        cells = jnp.concatenate(
            [
                lax.ppermute(tail, axis, [(i, (i + 1) % count) for i in range(ends)]),
                cells,
                lax.ppermute(head, axis, [((i + 1) % count, i) for i in range(ends)]),
            ],
            axis=dim,
        )
    return cells


def phase_list(offset):
    return [2.0 * math.pi * freq_hz * (STEP + offset) * TIME_STEP for freq_hz in FREQ_LIST]


def accumulate(running, field_in, offset):
    pieces = []
    for phase_angle in phase_list(offset):
        pieces.append(
            jnp.stack([field_in * math.cos(phase_angle), field_in * -math.sin(phase_angle)])
        )
    return running + jnp.stack(pieces)


def curl_field(h_field, rows_below, cols_left):
    magnet_x, magnet_y, magnet_z = (h_field[0], h_field[1], h_field[2])
    zero_plane = jnp.zeros_like(magnet_x[:1])
    x_below_z = jnp.concatenate([zero_plane, magnet_x[:-1]], 0)
    y_below_z = jnp.concatenate([zero_plane, magnet_y[:-1]], 0)
    y_below_x = jnp.concatenate([rows_below[0][:, None, :], magnet_y[:, :-1, :]], 1)
    z_below_x = jnp.concatenate([rows_below[1][:, None, :], magnet_z[:, :-1, :]], 1)
    x_below_y = jnp.concatenate([cols_left[0][:, :, None], magnet_x[:, :, :-1]], 2)
    z_below_y = jnp.concatenate([cols_left[1][:, :, None], magnet_z[:, :, :-1]], 2)
    curl_x = magnet_z - z_below_y - (magnet_y - y_below_z)
    curl_y = magnet_x - x_below_z - (magnet_z - z_below_x)
    curl_z = magnet_y - y_below_x - (magnet_x - x_below_y)
    return jnp.stack([curl_x, curl_y, curl_z])


def cross_product(left_vec, right_vec):
    return jnp.stack(
        [
            left_vec[:, 1] * right_vec[:, 2] - left_vec[:, 2] * right_vec[:, 1],
            left_vec[:, 2] * right_vec[:, 0] - left_vec[:, 0] * right_vec[:, 2],
            left_vec[:, 0] * right_vec[:, 1] - left_vec[:, 1] * right_vec[:, 0],
        ],
        1,
    )


def cross_flux(e_rows, h_rows):
    return 0.5 * (
        cross_product(e_rows[:, 0], h_rows[:, 0]) + cross_product(e_rows[:, 1], h_rows[:, 1])
    )


def lookup(material, material_table):
    kind_count = material_table.shape[1]
    flat_ids = material.reshape(1, -1)
    onehot = (
        lax.broadcasted_iota(jnp.int32, (kind_count, flat_ids.shape[1]), 0) == flat_ids
    ).astype(jnp.float32)
    coeffs = jnp.dot(
        material_table, onehot, precision=lax.Precision.HIGHEST, preferred_element_type=jnp.float32
    )
    return coeffs.reshape((4,) + material.shape)


def band_matrix(count, half_width):
    row_ids = lax.broadcasted_iota(jnp.int32, (count, count + 2 * half_width), 0)
    col_ids = lax.broadcasted_iota(jnp.int32, (count, count + 2 * half_width), 1)
    return ((col_ids >= row_ids) & (col_ids < row_ids + 2 * half_width)).astype(jnp.float32)


def pick_rows(values, index, lo_width):
    row_count = values.shape[0]
    hi_count = values.shape[1] // lo_width
    table = (
        values.reshape(row_count, hi_count, lo_width)
        .transpose(1, 0, 2)
        .reshape(hi_count, row_count * lo_width)
    )
    total = index.shape[0]
    block_len = math.gcd(total, 1024)
    hi_ids = (index // lo_width).reshape(-1, block_len)
    lo_ids = (index % lo_width).reshape(-1, block_len)
    lanes = lax.broadcasted_iota(jnp.int32, (1, 1, lo_width), 2)

    def one_block(pair):
        hi_block, lo_block = pair
        rows = jnp.take(table, hi_block, axis=0).reshape(block_len, row_count, lo_width)
        chosen = lo_block[:, None, None] == lanes
        return jnp.sum(jnp.where(chosen, rows, 0.0), axis=2)

    picked = lax.map(one_block, (hi_ids, lo_ids))
    return picked.reshape(total, row_count).T


def spread_rows(density, index, hi_count, lo_width):
    freq_count = density.shape[0]
    total = index.shape[0]
    first = density.astype(jnp.bfloat16)
    rest = density - lax.optimization_barrier(first).astype(jnp.float32)
    second = rest.astype(jnp.bfloat16)
    rest = rest - lax.optimization_barrier(second).astype(jnp.float32)
    third = rest.astype(jnp.bfloat16)
    split_parts = jnp.stack([first, second, third]).transpose(2, 0, 1)
    block_len = math.gcd(total, 2048)
    block_count = total // block_len
    part_blocks = split_parts.reshape(block_count, block_len, 3, freq_count)
    hi_blocks = (index // lo_width).reshape(block_count, block_len)
    lo_blocks = (index % lo_width).reshape(block_count, block_len)

    def add_block(carry, inputs):
        part_block, hi_block, lo_block = inputs
        hi_table = (
            lax.broadcasted_iota(jnp.int32, (hi_count, block_len), 0) == hi_block[None, :]
        ).astype(jnp.bfloat16)
        lo_table = (
            lo_block[:, None] == lax.broadcasted_iota(jnp.int32, (block_len, lo_width), 1)
        ).astype(jnp.bfloat16)
        spread = (part_block[:, :, :, None] * lo_table[:, None, None, :]).reshape(
            block_len, 3 * freq_count * lo_width
        )
        return (carry + jnp.dot(hi_table, spread, preferred_element_type=jnp.float32), None)

    start = jnp.zeros((hi_count, 3 * freq_count * lo_width), jnp.float32)
    summed, unused = lax.scan(add_block, start, (part_blocks, hi_blocks, lo_blocks))
    summed = summed.reshape(hi_count, 3, freq_count, lo_width)
    joined = summed[:, 0] + summed[:, 1] + summed[:, 2]
    return joined.transpose(1, 0, 2)


def send_rows(payload):
    return lax.all_to_all(payload, ("gy", "gx"), split_axis=1, concat_axis=1, tiled=True)


def shards(
    e_field,
    h_field,
    j_field,
    material,
    material_table,
    dft_e,
    dft_h,
    skin_cell,
    counts,
    patch_slot,
    area,
):
    magnet_x, magnet_y, magnet_z = (h_field[0], h_field[1], h_field[2])
    rows_below = shifted(jnp.stack([magnet_y[:, -1, :], magnet_z[:, -1, :]]), "gy", 1)
    cols_left = shifted(jnp.stack([magnet_x[:, :, -1], magnet_z[:, :, -1]]), "gx", 1)
    coeffs = lookup(material, material_table)
    curl_h = curl_field(h_field, rows_below, cols_left)
    e_next = coeffs[0] * e_field + coeffs[1] * (curl_h - j_field)
    j_next = coeffs[2] * j_field + coeffs[3] * (e_next - e_field)
    dft_e_next = accumulate(dft_e, e_next, 0.0)
    dft_h_next = accumulate(dft_h, h_field, 0.5)
    freq_count = dft_e.shape[0]
    blocks = skin_cell.shape[1]
    slot_count = skin_cell.shape[2]
    col_width = e_field.shape[3]
    skin_index = skin_cell.reshape(-1)
    live_mask = (
        lax.broadcasted_iota(jnp.int32, (blocks, slot_count), 1) < counts.reshape(blocks, 1)
    ).astype(jnp.float32)
    both_spectra = jnp.concatenate(
        [dft_e_next.reshape(6 * freq_count, -1), dft_h_next.reshape(6 * freq_count, -1)], 0
    )
    both_rows = (
        pick_rows(both_spectra, skin_index, col_width).reshape(12 * freq_count, blocks, slot_count)
        * live_mask
    )
    spectral_shape = (freq_count, 2, 3, blocks, slot_count)
    arrived = send_rows(both_rows)
    flux_rows = cross_flux(
        arrived[: 6 * freq_count].reshape(spectral_shape),
        arrived[6 * freq_count :].reshape(spectral_shape),
    )
    flux_rows = flux_rows.reshape(freq_count, 3, blocks * slot_count)
    rows_u = area.shape[1]
    cols_v = area.shape[2]
    patch_index = patch_slot.reshape(-1)
    area_rows = pick_rows(area.reshape(3, -1), patch_index, cols_v)
    density = (
        area_rows[0] * flux_rows[:, 0]
        + area_rows[1] * flux_rows[:, 1]
        + area_rows[2] * flux_rows[:, 2]
    )
    point_density = spread_rows(density, patch_index, rows_u, cols_v)
    padded = with_halo(point_density, (("gy", 1),), HALF)
    strip_sum = jnp.einsum(
        "ij,fjv->fiv",
        band_matrix(rows_u, HALF),
        padded,
        precision=lax.Precision.HIGHEST,
        preferred_element_type=jnp.float32,
    )
    padded_cols = with_halo(strip_sum, (("gx", 2),), HALF)
    square_sum = jnp.einsum(
        "fuj,ij->fui",
        padded_cols,
        band_matrix(cols_v, HALF),
        precision=lax.Precision.HIGHEST,
        preferred_element_type=jnp.float32,
    )
    avg_density = square_sum / (4.0 * HALF * HALF)
    return (e_next, j_next, dft_e_next, dft_h_next, point_density, avg_density)


def solution(mesh):
    placed = (
        P(None, None, "gy", "gx"),
        P(None, None, "gy", "gx"),
        P(None, None, "gy", "gx"),
        P(None, "gy", "gx"),
        P(),
        P(None, None, None, None, "gy", "gx"),
        P(None, None, None, None, "gy", "gx"),
        P(("gy", "gx"), None, None),
        P(("gy", "gx"), None),
        P(("gy", "gx"), None, None),
        P(None, "gy", "gx"),
    )
    return jax.shard_map(
        shards,
        mesh=mesh,
        in_specs=placed,
        out_specs=(
            P(None, None, "gy", "gx"),
            P(None, None, "gy", "gx"),
            P(None, None, None, None, "gy", "gx"),
            P(None, None, None, None, "gy", "gx"),
            P(None, "gy", "gx"),
            P(None, "gy", "gx"),
        ),
        check_vma=False,
    )
```

profile of v0, /device:TPU:21, one launch (start us, length us, event | category | flops | bytes accessed | tf_op | source)
XLA Modules:
  0.0 426.0 jit_solution(9073702211364596190)
XLA Ops:
  2.1 3.1 collective-permute-start
  6.7 4.0 collective-permute-start.1
  18.5 53.9 %while.33 = (s32[]{:T(128)}, f32[4,1024,3]{1,2,0:T(4,128)}, s32[4,1024]{1,0:T(4,128)}, s32[4,1024]{1,0:T(4,128)}, f32[256,768]{1,0:T(8,128)S(1)}, /*index=5*/s32[]{:T(128)}) while((s32[]{:T(128)}, f32[4,1024,3]{1,2,0:T(4,128)}, s32[4,1024]{1,0:T(4,128)}, s32[4,1024]{1,0:T(4,128)}, f32[256,768]{1,0:T(8,128)S(1)}, ...), condition=%wide.region_2.3_spmd.clone, body=%wide.region_0.2_spmd.clone.sunk | while | flops 2628610 | bytes 16337485 | solution.py:122
  19.4 5.3 %gather_fusion = f32[1024,768]{1,0:T(8,128)} fusion(f32[256,768]{1,0:T(8,128)S(1)} %get-tuple-element.549, s32[1024]{0:T(1024)S(1)} %broadcast_clamp_fusion.4), kind=kCustom, calls=%fused_computation.clone.clone.1 | custom fusion | bytes 6295552 | tf_op jit(solution)/shard_map/while/body/eval_jaxpr/jit(_take)/gather | solution.py:118
  24.7 3.6 copy.395
  29.2 2.4 select_reduce_fusion.4
  32.9 5.3 %gather_fusion = f32[1024,768]{1,0:T(8,128)} fusion(f32[256,768]{1,0:T(8,128)S(1)} %get-tuple-element.549, s32[1024]{0:T(1024)S(1)} %broadcast_clamp_fusion.4), kind=kCustom, calls=%fused_computation.clone.clone.1 | custom fusion | bytes 6295552 | tf_op jit(solution)/shard_map/while/body/eval_jaxpr/jit(_take)/gather | solution.py:118
  38.2 3.6 copy.395
  42.6 2.4 select_reduce_fusion.4
  46.3 5.3 %gather_fusion = f32[1024,768]{1,0:T(8,128)} fusion(f32[256,768]{1,0:T(8,128)S(1)} %get-tuple-element.549, s32[1024]{0:T(1024)S(1)} %broadcast_clamp_fusion.4), kind=kCustom, calls=%fused_computation.clone.clone.1 | custom fusion | bytes 6295552 | tf_op jit(solution)/shard_map/while/body/eval_jaxpr/jit(_take)/gather | solution.py:118
  51.6 3.6 copy.395
  56.0 2.4 select_reduce_fusion.4
  59.7 5.3 %gather_fusion = f32[1024,768]{1,0:T(8,128)} fusion(f32[256,768]{1,0:T(8,128)S(1)} %get-tuple-element.549, s32[1024]{0:T(1024)S(1)} %broadcast_clamp_fusion.4), kind=kCustom, calls=%fused_computation.clone.clone.1 | custom fusion | bytes 6295552 | tf_op jit(solution)/shard_map/while/body/eval_jaxpr/jit(_take)/gather | solution.py:118
  65.0 3.6 copy.395
  69.5 2.4 select_reduce_fusion.4
  78.5 1.7 copy.344
  80.2 1.7 copy.345
  82.0 1.8 copy.298
  83.7 1.8 copy.300
  86.8 2.2 copy.310
  89.0 1.7 copy.311
  91.6 6.0 %copy.315 = f32[3,2,3,4,64,128]{4,3,5,2,1,0:T(4,128)} copy(f32[3,2,3,4,64,128]{5,4,3,2,1,0:T(8,128)} %param.22) | data formatting | bytes 4718592 | tf_op args[5]
  99.3 1.6 fusion.35
  100.9 1.8 fusion.32
  103.8 2.2 multiply_bitcast_fusion.4
  107.2 3.2 maximum_add_fusion
  110.4 6.0 %copy.337 = f32[3,2,3,4,64,128]{5,4,3,2,1,0:T(8,128)} copy(f32[3,2,3,4,64,128]{4,3,5,2,1,0:T(4,128)} %maximum_add_fusion) | data formatting | bytes 4718592
  116.4 4.6 %maximum_bitcast_fusion = f32[256,36,128]{2,0,1:T(8,128)} fusion(f32[18,256,128]{2,1,0:T(8,128)S(1)} %bitcast.240, f32[18,256,128]{2,1,0:T(8,128)} %bitcast.241), kind=kLoop, calls=%fused_computation.32 | loop fusion | flops 1179648 | bytes 9437184 | tf_op jit(solution)/shard_map/transpose | solution.py:107
  121.1 6.1 %copy.319 = f32[256,36,128]{0,2,1:T(8,128)} copy(f32[256,36,128]{2,0,1:T(8,128)} %maximum_bitcast_fusion) | data formatting | bytes 9437184 | tf_op jit(solution)/shard_map/transpose | solution.py:107
  127.1 6.1 %copy.320 = f32[256,4608]{1,0:T(8,128)} copy(f32[256,4608]{0,1:T(8,128)} %bitcast.238) | data formatting | bytes 9437184
  133.3 205.3 %while.34 = (s32[]{:T(128)}, f32[4,1024,36]{1,0,2:T(4,128)S(1)}, s32[4,1024]{1,0:T(4,128)}, s32[4,1024]{1,0:T(4,128)}, f32[256,4608]{1,0:T(8,128)}, /*index=5*/s32[]{:T(128)}, s32[]{:T(128)}) while((s32[]{:T(128)}, f32[4,1024,36]{1,0,2:T(4,128)S(1)}, s32[4,1024]{1,0:T(4,128)}, s32[4,1024]{1,0:T(4,128)}, f32[256,4608]{1,0:T(8,128)}, ...), condition=%wide.region_5.6_spmd.clone, body=%wide.region_3.5_spmd.clone.sunk | while | flops 14260226 | bytes 95414352 | solution.py:122
  134.0 18.9 %gather_fusion.1 = f32[1024,4608]{1,0:T(8,128)} fusion(f32[256,4608]{1,0:T(8,128)} %get-tuple-element.530, s32[1024]{0:T(1024)S(1)} %broadcast_clamp_fusion.5), kind=kCustom, calls=%fused_computation.1.clone.clone.1 | custom fusion | bytes 37752832 | tf_op jit(solution)/shard_map/while/body/eval_jaxpr/jit(_take)/gather | solution.py:118
  152.9 18.7 %copy.396 = f32[1024,4608]{0,1:T(8,128)} copy(f32[1024,4608]{1,0:T(8,128)} %gather_fusion.1) | data formatting | bytes 37748736 | tf_op jit(solution)/shard_map/while/body/eval_jaxpr/jit(_take)/gather | solution.py:118
  172.4 9.0 %select_reduce_fusion.5 = f32[1024,36]{0,1:T(8,128)S(1)} fusion(f32[1024,36,128]{0,2,1:T(8,128)} %bitcast.233, pred[1024]{0:T(1024)(128)(4,1)S(1)} %compare_and_fusion.5, pred[1024,128]{0,1:T(8,128)(4,1)S(1)} %iota_compare_fusion.14), kind=kLoop, calls=%fused_computation.13.clone.1 | loop fusion | flops 14118912 | bytes 19153920 | tf_op jit(solution)/shard_map/while/body/eval_jaxpr/reduce_sum | solution.py:120
  181.6 3.0 dynamic_update_slice.14
  185.4 18.9 %gather_fusion.1 = f32[1024,4608]{1,0:T(8,128)} fusion(f32[256,4608]{1,0:T(8,128)} %get-tuple-element.530, s32[1024]{0:T(1024)S(1)} %broadcast_clamp_fusion.5), kind=kCustom, calls=%fused_computation.1.clone.clone.1 | custom fusion | bytes 37752832 | tf_op jit(solution)/shard_map/while/body/eval_jaxpr/jit(_take)/gather | solution.py:118
  204.2 18.7 %copy.396 = f32[1024,4608]{0,1:T(8,128)} copy(f32[1024,4608]{1,0:T(8,128)} %gather_fusion.1) | data formatting | bytes 37748736 | tf_op jit(solution)/shard_map/while/body/eval_jaxpr/jit(_take)/gather | solution.py:118
  223.7 9.0 %select_reduce_fusion.5 = f32[1024,36]{0,1:T(8,128)S(1)} fusion(f32[1024,36,128]{0,2,1:T(8,128)} %bitcast.233, pred[1024]{0:T(1024)(128)(4,1)S(1)} %compare_and_fusion.5, pred[1024,128]{0,1:T(8,128)(4,1)S(1)} %iota_compare_fusion.14), kind=kLoop, calls=%fused_computation.13.clone.1 | loop fusion | flops 14118912 | bytes 19153920 | tf_op jit(solution)/shard_map/while/body/eval_jaxpr/reduce_sum | solution.py:120
  232.9 3.0 dynamic_update_slice.14
  236.7 18.9 %gather_fusion.1 = f32[1024,4608]{1,0:T(8,128)} fusion(f32[256,4608]{1,0:T(8,128)} %get-tuple-element.530, s32[1024]{0:T(1024)S(1)} %broadcast_clamp_fusion.5), kind=kCustom, calls=%fused_computation.1.clone.clone.1 | custom fusion | bytes 37752832 | tf_op jit(solution)/shard_map/while/body/eval_jaxpr/jit(_take)/gather | solution.py:118
  255.6 18.7 %copy.396 = f32[1024,4608]{0,1:T(8,128)} copy(f32[1024,4608]{1,0:T(8,128)} %gather_fusion.1) | data formatting | bytes 37748736 | tf_op jit(solution)/shard_map/while/body/eval_jaxpr/jit(_take)/gather | solution.py:118
  275.1 9.0 %select_reduce_fusion.5 = f32[1024,36]{0,1:T(8,128)S(1)} fusion(f32[1024,36,128]{0,2,1:T(8,128)} %bitcast.233, pred[1024]{0:T(1024)(128)(4,1)S(1)} %compare_and_fusion.5, pred[1024,128]{0,1:T(8,128)(4,1)S(1)} %iota_compare_fusion.14), kind=kLoop, calls=%fused_computation.13.clone.1 | loop fusion | flops 14118912 | bytes 19153920 | tf_op jit(solution)/shard_map/while/body/eval_jaxpr/reduce_sum | solution.py:120
  284.2 3.0 dynamic_update_slice.14
  288.0 18.9 %gather_fusion.1 = f32[1024,4608]{1,0:T(8,128)} fusion(f32[256,4608]{1,0:T(8,128)} %get-tuple-element.530, s32[1024]{0:T(1024)S(1)} %broadcast_clamp_fusion.5), kind=kCustom, calls=%fused_computation.1.clone.clone.1 | custom fusion | bytes 37752832 | tf_op jit(solution)/shard_map/while/body/eval_jaxpr/jit(_take)/gather | solution.py:118
  306.9 18.7 %copy.396 = f32[1024,4608]{0,1:T(8,128)} copy(f32[1024,4608]{1,0:T(8,128)} %gather_fusion.1) | data formatting | bytes 37748736 | tf_op jit(solution)/shard_map/while/body/eval_jaxpr/jit(_take)/gather | solution.py:118
  326.4 9.0 %select_reduce_fusion.5 = f32[1024,36]{0,1:T(8,128)S(1)} fusion(f32[1024,36,128]{0,2,1:T(8,128)} %bitcast.233, pred[1024]{0:T(1024)(128)(4,1)S(1)} %compare_and_fusion.5, pred[1024,128]{0,1:T(8,128)(4,1)S(1)} %iota_compare_fusion.14), kind=kLoop, calls=%fused_computation.13.clone.1 | loop fusion | flops 14118912 | bytes 19153920 | tf_op jit(solution)/shard_map/while/body/eval_jaxpr/reduce_sum | solution.py:120
  335.6 3.0 dynamic_update_slice.14
  340.6 3.7 all-to-all-start
  344.4 14.9 %all-to-all-done = f32[36,32,128]{2,0,1:T(8,128)S(1)} async-done(((f32[36,32,128]{2,0,1:T(8,128)}), f32[36,32,128]{2,0,1:T(8,128)S(1)}, u32[]{:S(2)}, u32[]{:S(2)}) %all-to-all-start) | async-done | bytes 589856 | tf_op jit(solution)/shard_map/all_to_all | solution.py:162
  361.1 23.4 %while.35 = (s32[]{:T(128)}, f32[256,2304]{1,0:T(8,128)S(1)}, s32[2,2048]{1,0:T(2,128)S(1)}, bf16[2,2048,3,3]{1,3,2,0:T(4,128)(2,1)S(1)}, s32[2,2048]{1,0:T(2,128)S(1)}, /*index=5*/s32[]{:T(128)}, s32[]{:T(128)}) while((s32[]{:T(128)}, f32[256,2304]{1,0:T(8,128)S(1)}, s32[2,2048]{1,0:T(2,128)S(1)}, ...), condition=%wide.region_7.8_spmd.clone, body=%wide.region_6.7_spmd.clone.sunk | while | flops 2423390208 | bytes 25849952 | solution.py:155
  361.4 4.3 %broadcast_multiply_fusion.2 = bf16[2048,3,3,256]{0,3,2,1:T(8,128)(2,1)} fusion(bf16[2048,256]{0,1:T(8,128)(2,1)S(1)} %fusion.71, bf16[2048,3,3]{0,2,1:T(4,128)(2,1)S(1)} %dynamic-slice_bitcast_fusion.2), kind=kLoop, calls=%fused_computation.21.clone.1 | loop fusion | flops 4718592 | bytes 10522624 | tf_op jit(solution)/shard_map/while/body/eval_jaxpr/mul | solution.py:149
  365.7 7.1 %convolution_add_fusion.2 = f32[256,2304]{1,0:T(8,128)S(1)} fusion(bf16[2048,2304]{0,1:T(8,128)(2,1)} %bitcast.235, f32[256,2304]{1,0:T(8,128)S(1)} %get-tuple-element.559, pred[]{:T(512)S(6)} %compare.18, s32[2048]{0:T(1024)S(1)} %bitcast.272), kind=kOutput, calls=%fused_computation.22.clone.1 | convolution fusion | flops 2417623040 | bytes 14163969 | tf_op jit(solution)/shard_map/while/body/eval_jaxpr/dot_general | solution.py:152
  373.1 4.3 %broadcast_multiply_fusion.2 = bf16[2048,3,3,256]{0,3,2,1:T(8,128)(2,1)} fusion(bf16[2048,256]{0,1:T(8,128)(2,1)S(1)} %fusion.71, bf16[2048,3,3]{0,2,1:T(4,128)(2,1)S(1)} %dynamic-slice_bitcast_fusion.2), kind=kLoop, calls=%fused_computation.21.clone.1 | loop fusion | flops 4718592 | bytes 10522624 | tf_op jit(solution)/shard_map/while/body/eval_jaxpr/mul | solution.py:149
  377.4 7.1 %convolution_add_fusion.2 = f32[256,2304]{1,0:T(8,128)S(1)} fusion(bf16[2048,2304]{0,1:T(8,128)(2,1)} %bitcast.235, f32[256,2304]{1,0:T(8,128)S(1)} %get-tuple-element.559, pred[]{:T(512)S(6)} %compare.18, s32[2048]{0:T(1024)S(1)} %bitcast.272), kind=kOutput, calls=%fused_computation.22.clone.1 | convolution fusion | flops 2417623040 | bytes 14163969 | tf_op jit(solution)/shard_map/while/body/eval_jaxpr/dot_general | solution.py:152
  385.9 2.0 copy.331
  392.7 4.1 collective-permute-start.2
  396.8 1.9 collective-permute-start.3
  398.8 2.0 collective-permute-done.2
  400.7 4.4 %collective-permute-done.3 = f32[3,100,256]{2,1,0:T(8,128)S(1)} collective-permute-done((f32[3,100,256]{2,1,0:T(8,128)S(1)}, f32[3,100,256]{2,1,0:T(8,128)S(1)}, u32[]{:S(2)}, u32[]{:S(2)}) %collective-permute-start.3) | collective-permute-done | bytes 307232 | tf_op jit(solution)/shard_map/ppermute | solution.py:32
  407.4 3.1 collective-permute-start.4
  410.4 3.1 collective-permute-start.5
  415.6 3.9 collective-permute-done.4
  419.5 4.2 collective-permute-done.5
  423.7 2.3 fusion.22
  (193 shorter events, 52.9 us)
Async XLA Ops:
  0.6 13.5 %copy-start = (f32[4,32]{1,0:T(4,128)S(1)}, f32[4,32]{1,0:T(4,128)}, u32[]{:S(2)}) copy-start(f32[4,32]{1,0:T(4,128)} %param.21) | copy-start | bytes 1540
  0.6 10.1 %copy-start.10 = (f32[3,4,64,128]{3,2,1,0:T(8,128)S(1)}, f32[3,4,64,128]{3,2,1,0:T(8,128)}, u32[]{:S(2)}) copy-start(f32[3,4,64,128]{3,2,1,0:T(8,128)} %param.18) | copy-start | bytes 1179652
  2.1 12.1 %copy-start.7 = (f32[1,4,64,128]{2,1,3,0:T(4,128)}, f32[1,4,64,128]{2,1,3,0:T(4,128)S(1)}, u32[]{:S(2)}) copy-start(f32[1,4,64,128]{2,1,3,0:T(4,128)S(1)} %copy.342) | copy-start | bytes 393220
  2.1 95.4 %collective-permute-start = (f32[2,4,64]{2,1,0:T(4,128)S(1)}, f32[2,4,64]{2,1,0:T(4,128)S(1)}, u32[]{:S(2)}, u32[]{:S(2)}) collective-permute-start(f32[2,4,64]{2,1,0:T(4,128)S(1)} %pad_maximum_fusion), channel_id=1, source_target_pairs={{0,1},{1,2},{2,3},{4,5},{5,6},{6,7},{8,9},{9,10},{10,11},{12,13},{... | collective-permute-start | bytes 6152 | tf_op jit(solution)/shard_map/ppermute | solution.py:19
  5.7 8.4 %copy-start.6 = (f32[1,4,64,128]{2,1,3,0:T(4,128)}, f32[1,4,64,128]{2,1,3,0:T(4,128)S(1)}, u32[]{:S(2)}) copy-start(f32[1,4,64,128]{2,1,3,0:T(4,128)S(1)} %copy.343) | copy-start | bytes 393220
  5.9 8.2 %copy-start.27 = (s32[4,64,128]{2,1,0:T(8,128)S(1)}, s32[4,64,128]{2,1,0:T(8,128)}, u32[]{:S(2)}) copy-start(s32[4,64,128]{2,1,0:T(8,128)} %param.20) | copy-start | bytes 393220
  6.7 90.9 %collective-permute-start.1 = (f32[2,4,128]{2,1,0:T(4,128)}, f32[2,4,128]{2,1,0:T(4,128)S(1)}, u32[]{:S(2)}, u32[]{:S(2)}) collective-permute-start(f32[2,4,128]{2,1,0:T(4,128)} %pad_maximum_fusion.1), channel_id=1, source_target_pairs={{0,4},{4,8},{8,12},{12,16},{16,20},{20,24},{24,28},{1,5},{5,9},{9,... | collective-permute-start | bytes 12296 | tf_op jit(solution)/shard_map/ppermute | solution.py:19
  12.8 3.8 copy-start.25
  12.9 4.4 %copy-start.23 = (s32[1,32,128]{2,1,0:T(8,128)S(1)}, s32[1,32,128]{2,1,0:T(8,128)}, u32[]{:S(2)}) copy-start(s32[1,32,128]{2,1,0:T(8,128)} %param.26) | copy-start | bytes 49156
  12.9 5.1 %copy-start.19 = (f32[3,256,256]{2,1,0:T(8,128)S(1)}, f32[3,256,256]{2,1,0:T(8,128)}, u32[]{:S(2)}) copy-start(f32[3,256,256]{2,1,0:T(8,128)} %param.27) | copy-start | bytes 2359300
  18.5 55.3 %copy-start.14 = (f32[1,3,4,64,128]{4,3,2,1,0:T(8,128)S(1)}, f32[1,3,4,64,128]{4,3,2,1,0:T(8,128)}, u32[]{:S(2)}) copy-start(f32[1,3,4,64,128]{4,3,2,1,0:T(8,128)} %get-tuple-element.365) | copy-start | bytes 1179652
  72.4 2.5 copy-start.11
  75.0 0.7 copy-start.26
  75.5 41.0 %copy-start.2 = (f32[3,2,3,4,64,128]{5,4,3,2,1,0:T(8,128)}, f32[3,2,3,4,64,128]{5,4,3,2,1,0:T(8,128)S(1)}, u32[]{:S(2)}) copy-start(f32[3,2,3,4,64,128]{5,4,3,2,1,0:T(8,128)S(1)} %maximum_add_fusion.1) | copy-start | bytes 7077892
  99.3 3.5 copy-start.5
  99.3 3.5 copy-start.15
  99.3 3.5 copy-start.16
  102.7 1.0 copy-start.17
  102.8 1.0 copy-start.18
  103.4 2.6 copy-start.3
  103.8 3.4 slice-start
  105.9 1.3 slice-start.1
  127.1 6.1 %copy-start.20 = (f32[4,1024,36]{1,0,2:T(4,128)S(1)}, f32[4,1024,36]{1,0,2:T(4,128)}, u32[]{:S(2)}) copy-start(f32[4,1024,36]{1,0,2:T(4,128)} %custom-call.6) | copy-start | bytes 1769476
  338.6 0.7 copy-start.21
  339.1 5.1 %copy-start.22 = (s32[2,2048]{1,0:T(2,128)S(1)}, s32[2,2048]{1,0:T(2,128)}, u32[]{:S(2)}) copy-start(s32[2,2048]{1,0:T(2,128)} %reshape.398) | copy-start | bytes 49156
  339.2 5.2 %copy-start.24 = (f32[4,1024,3]{1,2,0:T(4,128)S(1)}, f32[4,1024,3]{1,2,0:T(4,128)}, u32[]{:S(2)}) copy-start(f32[4,1024,3]{1,2,0:T(4,128)} %get-tuple-element.97) | copy-start | bytes 147460
  340.6 18.7 %all-to-all-start = ((f32[36,32,128]{2,0,1:T(8,128)}), f32[36,32,128]{2,0,1:T(8,128)S(1)}, u32[]{:S(2)}, u32[]{:S(2)}) async-start(f32[36,32,128]{2,0,1:T(8,128)} %copy.322), calls=%async_computation | async-start | bytes 1310720 | tf_op jit(solution)/shard_map/all_to_all | solution.py:162
  359.4 1.7 copy-start.12
  384.5 1.4 copy-start.13
  392.6 14.7 %copy-start.9 = (f32[3,256,256]{2,1,0:T(8,128)}, f32[3,256,256]{2,1,0:T(8,128)S(1)}, u32[]{:S(2)}) copy-start(f32[3,256,256]{2,1,0:T(8,128)S(1)} %add_bitcast_fusion) | copy-start | bytes 2359300
  392.6 20.9 %copy-start.4 = (f32[3,4,64,128]{2,1,3,0:T(4,128)S(1)}, f32[3,4,64,128]{2,1,3,0:T(4,128)}, u32[]{:S(2)}) copy-start(f32[3,4,64,128]{2,1,3,0:T(4,128)} %copy-done.3) | copy-start | bytes 1179652
  392.7 8.0 %collective-permute-start.2 = (f32[3,100,256]{2,1,0:T(8,128)S(1)}, f32[3,100,256]{2,1,0:T(8,128)S(1)}, u32[]{:S(2)}, u32[]{:S(2)}) collective-permute-start(f32[3,100,256]{2,1,0:T(8,128)S(1)} %get-tuple-element.349), channel_id=1, source_target_pairs={{0,4},{4,8},{8,12},{12,16},{16,20},{20,24},{24,28},{1,5},{5,9},{9,... | collective-permute-start | bytes 921608 | tf_op jit(solution)/shard_map/ppermute | solution.py:30
  396.8 8.3 %collective-permute-start.3 = (f32[3,100,256]{2,1,0:T(8,128)S(1)}, f32[3,100,256]{2,1,0:T(8,128)S(1)}, u32[]{:S(2)}, u32[]{:S(2)}) collective-permute-start(f32[3,100,256]{2,1,0:T(8,128)S(1)} %get-tuple-element.350), channel_id=1, source_target_pairs={{4,0},{8,4},{12,8},{16,12},{20,16},{24,20},{28,24},{5,1},{9,5},{13... | collective-permute-start | bytes 921608 | tf_op jit(solution)/shard_map/ppermute | solution.py:32
  398.8 15.8 %copy-start.8 = (f32[3,4,64,128]{2,1,3,0:T(4,128)S(1)}, f32[3,4,64,128]{2,1,3,0:T(4,128)}, u32[]{:S(2)}) copy-start(f32[3,4,64,128]{2,1,3,0:T(4,128)} %get-tuple-element.356) | copy-start | bytes 1179652
  407.4 12.2 %collective-permute-start.4 = (f32[3,256,100]{1,2,0:T(8,128)}, f32[3,256,100]{1,2,0:T(8,128)S(1)}, u32[]{:S(2)}, u32[]{:S(2)}) collective-permute-start(f32[3,256,100]{1,2,0:T(8,128)} %get-tuple-element.347), channel_id=1, source_target_pairs={{0,1},{1,2},{2,3},{4,5},{5,6},{6,7},{8,9},{9,10},{10,11},{12,13},{... | collective-permute-start | bytes 921608 | tf_op jit(solution)/shard_map/ppermute | solution.py:30
  410.4 15.6 %copy-start.1 = (f32[4,32]{1,0:T(4,128)S(1)}, f32[4,32]{1,0:T(4,128)}, u32[]{:S(2)}) copy-start(f32[4,32]{1,0:T(4,128)} %param.21) | copy-start | bytes 1540
  410.4 13.3 %collective-permute-start.5 = (f32[3,256,100]{1,2,0:T(8,128)S(1)}, f32[3,256,100]{1,2,0:T(8,128)S(1)}, u32[]{:S(2)}, u32[]{:S(2)}) collective-permute-start(f32[3,256,100]{1,2,0:T(8,128)S(1)} %get-tuple-element.348), channel_id=1, source_target_pairs={{1,0},{2,1},{3,2},{5,4},{6,5},{7,6},{9,8},{10,9},{11,10},{13,12},{... | collective-permute-start | bytes 921608 | tf_op jit(solution)/shard_map/ppermute | solution.py:32
where the time goes:
time: 433 us; the launch traced here: 426 us
  local copies, waits for them, and re-layouts  268 us (62%)
  other arithmetic  84.5 us (20%)
  waiting for transfers between devices  29.4 us (7%)
  starting transfers between devices  23.1 us (5%)
  matrix products  19.3 us (4%)
    gather x16, local copies, waits for them, and re-layouts, one_block(): jnp.take(table, hi_block, axis=0).reshape(block_len, row_count, lo_width)  186 us
    reduce_sum x8, other arithmetic, one_block(): return jnp.sum(jnp.where(chosen, rows, 0.0), axis=2)  45.4 us
    unnamed x83, local copies, waits for them, and re-layouts  34.5 us
    dynamic_update_slice x12, local copies, waits for them, and re-layouts, pick_rows(): picked = lax.map(one_block, (hi_ids, lo_ids))  15.2 us
    all_to_all x1, waiting for transfers between devices, send_rows(): lax.all_to_all(payload, ('gy', 'gx'), split_axis=1, concat_axis=1, tiled=...  14.9 us
    dot_general x2, matrix products, add_block(): jnp.dot(hi_table, spread, preferred_element_type=jnp.float32)  14.2 us
  transfers between devices with their start and end apart: 7, of which 5 were waited for; matrix products, arithmetic and copies ran while one was open for 21% of the time, Pallas kernels for 0%

commit v1 on v0

v1 whole, which is shorter than its diff:
```python
import math

import jax
import jax.numpy as jnp
from jax import lax
from jax.experimental import pallas as pl
from jax.experimental.pallas import tpu as pltpu
from jax.sharding import PartitionSpec as P

STEP = 1000
HALF = 100


FREQ_LIST = (28000000000.0, 39000000000.0, 60000000000.0)
TIME_STEP = 1.9e-13


def shifted(value, axis, steps):
    count = lax.axis_size(axis)
    leading, last = (max(0, -steps), min(count, count - steps))
    return lax.ppermute(value, axis, [(source, source + steps) for source in range(leading, last)])


def with_halo(cells, sides, width):
    for axis, dim in sides:
        count = lax.axis_size(axis)
        ends = count - 1
        head = lax.slice_in_dim(cells, 0, width, axis=dim)
        tail = lax.slice_in_dim(cells, cells.shape[dim] - width, cells.shape[dim], axis=dim)
        cells = jnp.concatenate(
            [
                lax.ppermute(tail, axis, [(i, (i + 1) % count) for i in range(ends)]),
                cells,
                lax.ppermute(head, axis, [((i + 1) % count, i) for i in range(ends)]),
            ],
            axis=dim,
        )
    return cells


def phase_list(offset):
    return [2.0 * math.pi * freq_hz * (STEP + offset) * TIME_STEP for freq_hz in FREQ_LIST]


def shift_of(size):
    return size.bit_length() - 1


def iota0(rows, cols):
    return lax.broadcasted_iota(jnp.int32, (rows, cols), 0)


def split_two(values):
    first = values.astype(jnp.bfloat16)
    return first, (values - first.astype(jnp.float32)).astype(jnp.bfloat16)


def field_kernel(
    h_ref, e_ref, j_ref, mat_ref, table_ref, rows_ref, cols_ref, de_ref, dh_ref,
    en_ref, jn_ref, den_ref, dhn_ref, flux_ref, table_s, cols_s,
):
    step = pl.program_id(0)
    per, rx, cy = mat_ref.shape
    planes = h_ref.shape[1]
    freqs = de_ref.shape[0]
    table_s[...] = jnp.zeros_like(table_s)
    table_s[0:4, 0 : table_ref.shape[1]] = table_ref[...]
    cols_s[...] = jnp.zeros_like(cols_s)
    cols_s[:, 0:rx] = cols_ref[...]
    first_row = iota0(rx, cy) == 0
    first_col = lax.broadcasted_iota(jnp.int32, (rx, cy), 1) == 0
    cos_e = [math.cos(a) for a in phase_list(0.0)]
    sin_e = [-math.sin(a) for a in phase_list(0.0)]
    cos_h = [math.cos(a) for a in phase_list(0.5)]
    sin_h = [-math.sin(a) for a in phase_list(0.5)]

    def row_below(value, comp, z):
        edge = jnp.broadcast_to(rows_ref[comp, pl.ds(z, 1), :], (rx, cy))
        return jnp.where(first_row, edge, pltpu.roll(value, 1, 0))

    def col_below(value, comp, z):
        line = cols_s[pl.ds(comp * planes + z, 1), :]
        edge = jnp.broadcast_to(line, (cy, cy)).T[:rx]
        return jnp.where(first_col, edge, pltpu.roll(value, 1, 1))

    for k in range(per):
        z = step * per + k
        below = jnp.maximum(z - 1, 0)
        keep = jnp.where(z > 0, 1.0, 0.0)
        hx, hy, hz = (h_ref[c, z] for c in range(3))
        curl = (
            (hz - col_below(hz, 1, z)) - (hy - h_ref[1, below] * keep),
            (hx - h_ref[0, below] * keep) - (hz - row_below(hz, 1, z)),
            (hy - row_below(hy, 0, z)) - (hx - col_below(hx, 0, z)),
        )
        kinds = mat_ref[k]
        coeffs = [
            jnp.take_along_axis(
                jnp.broadcast_to(table_s[r : r + 1, :], (rx, cy)), kinds, axis=1,
                mode="promise_in_bounds",
            )
            for r in range(4)
        ]
        en = []
        for c in range(3):
            e_old, j_old = e_ref[c, k], j_ref[c, k]
            e_new = coeffs[0] * e_old + coeffs[1] * (curl[c] - j_old)
            en_ref[c, k] = e_new
            jn_ref[c, k] = coeffs[2] * j_old + coeffs[3] * (e_new - e_old)
            en.append(e_new)
        h_now = (hx, hy, hz)
        for f in range(freqs):
            spectra = []
            for part in range(2):
                e_scale = (cos_e, sin_e)[part][f]
                h_scale = (cos_h, sin_h)[part][f]
                e_part = [de_ref[f, part, c, k] + en[c] * e_scale for c in range(3)]
                h_part = [dh_ref[f, part, c, k] + h_now[c] * h_scale for c in range(3)]
                for c in range(3):
                    den_ref[f, part, c, k] = e_part[c]
                    dhn_ref[f, part, c, k] = h_part[c]
                spectra.append((e_part, h_part))
            for c in range(3):
                a, b = (c + 1) % 3, (c + 2) % 3
                real, imag = [ep[a] * hp[b] - ep[b] * hp[a] for ep, hp in spectra]
                high, low = split_two(0.5 * (real + imag))
                flux_ref[f * 3 + c, k * rx : (k + 1) * rx, 0:cy] = high
                flux_ref[f * 3 + c, k * rx : (k + 1) * rx, cy : 2 * cy] = low


def update_fields(h, e, j, material, table, rows, cols, dft_e, dft_h):
    _, planes, rx, cy = h.shape
    freqs = dft_e.shape[0]
    per = 2 if planes % 2 == 0 else 1
    field_block = pl.BlockSpec((3, per, rx, cy), lambda s: (0, s, 0, 0))
    dft_block = pl.BlockSpec((freqs, 2, 3, per, rx, cy), lambda s: (0, 0, 0, s, 0, 0))
    return pl.pallas_call(
        field_kernel,
        grid=(planes // per,),
        in_specs=[
            pl.BlockSpec(h.shape, lambda s: (0, 0, 0, 0)),
            field_block,
            field_block,
            pl.BlockSpec((per, rx, cy), lambda s: (s, 0, 0)),
            pl.BlockSpec(table.shape, lambda s: (0, 0)),
            pl.BlockSpec(rows.shape, lambda s: (0, 0, 0)),
            pl.BlockSpec(cols.shape, lambda s: (0, 0)),
            dft_block,
            dft_block,
        ],
        out_specs=[
            field_block, field_block, dft_block, dft_block,
            pl.BlockSpec((3 * freqs, per * rx, 2 * cy), lambda s: (0, s, 0)),
        ],
        out_shape=[
            jax.ShapeDtypeStruct(e.shape, jnp.float32),
            jax.ShapeDtypeStruct(j.shape, jnp.float32),
            jax.ShapeDtypeStruct(dft_e.shape, jnp.float32),
            jax.ShapeDtypeStruct(dft_h.shape, jnp.float32),
            jax.ShapeDtypeStruct((3 * freqs, planes * rx, 2 * cy), jnp.bfloat16),
        ],
        scratch_shapes=[
            pltpu.VMEM((8, cy), jnp.float32),
            pltpu.VMEM((2 * planes, cy), jnp.float32),
        ],
        compiler_params=pltpu.CompilerParams(vmem_limit_bytes=40 << 20),
        cost_estimate=pl.CostEstimate(flops=10 * dft_e.size, bytes_accessed=14 << 20, transcendentals=0),
    )(h, e, j, material, table, rows, cols, dft_e, dft_h)


def area_kernel(area_ref, patch_ref, skin_ref, counts_ref, out_ref, live_ref, split_s):
    comps, pu, pv = area_ref.shape
    blocks, cap = patch_ref.shape
    for c in range(comps):
        high, low = split_two(area_ref[c])
        split_s[c, :, 0:pv] = high
        split_s[c, :, pv : 2 * pv] = low
    slots = lax.broadcasted_iota(jnp.int32, (1, cap), 1)

    def pair(t, carry):
        ids = jnp.concatenate([patch_ref[pl.ds(2 * t + i, 1), :] for i in range(2)], 1)
        low = (iota0(pv, 2 * cap) == (ids & (pv - 1))).astype(jnp.float32).astype(jnp.bfloat16)
        both = jnp.concatenate([low, low], 0)
        hit = iota0(pu, 2 * cap) == (ids >> shift_of(pv))
        for c in range(comps):
            rows = jnp.dot(split_s[c], both, preferred_element_type=jnp.float32)
            value = jnp.sum(jnp.where(hit, rows, 0.0), axis=0, keepdims=True)
            for i in range(2):
                out_ref[c, pl.ds(2 * t + i, 1), :] = value[:, i * cap : (i + 1) * cap]
        for i in range(2):
            d = 2 * t + i
            live_ref[pl.ds(d, 1), :] = jnp.where(
                slots < counts_ref[0, d], skin_ref[pl.ds(d, 1), :], -1
            )
        return carry

    lax.fori_loop(0, blocks // 2, pair, 0)


def gather_area(area, patch, skin, counts):
    vmem = pl.BlockSpec(memory_space=pltpu.VMEM)
    blocks, cap = patch.shape
    return pl.pallas_call(
        area_kernel,
        in_specs=[vmem, vmem, vmem, pl.BlockSpec(memory_space=pltpu.SMEM)],
        out_specs=[vmem, vmem],
        out_shape=[
            jax.ShapeDtypeStruct((area.shape[0],) + patch.shape, jnp.float32),
            jax.ShapeDtypeStruct(skin.shape, jnp.int32),
        ],
        scratch_shapes=[
            pltpu.VMEM((area.shape[0], area.shape[1], 2 * area.shape[2]), jnp.bfloat16)
        ],
        compiler_params=pltpu.CompilerParams(vmem_limit_bytes=40 << 20),
        cost_estimate=pl.CostEstimate(
            flops=4 * area.size * blocks * cap, bytes_accessed=4 * area.size, transcendentals=0
        ),
    )(area, patch, skin, counts)


def flux_pair(flux_ref, live_ref, t):
    rows, hi_count, two_lo = flux_ref.shape
    lo_count = two_lo // 2
    ids = jnp.concatenate([live_ref[pl.ds(2 * t + i, 1), :] for i in range(2)], 1)
    width = ids.shape[1]
    low = (iota0(lo_count, width) == (ids & (lo_count - 1))).astype(jnp.float32)
    low = low.astype(jnp.bfloat16)
    both = jnp.concatenate([low, low], 0)
    hit = iota0(hi_count, width) == (ids >> shift_of(lo_count))
    picked = []
    for r in range(rows):
        part = jnp.dot(flux_ref[r], both, preferred_element_type=jnp.float32)
        picked.append(jnp.sum(jnp.where(hit, part, 0.0), axis=0, keepdims=True))
    return picked


def flux_kernel(flux_ref, live_ref, out_ref):
    cap = live_ref.shape[1]

    def pair(t, carry):
        for r, value in enumerate(flux_pair(flux_ref, live_ref, t)):
            for i in range(2):
                out_ref[r, pl.ds(2 * t + i, 1), :] = value[:, i * cap : (i + 1) * cap]
        return carry

    lax.fori_loop(0, live_ref.shape[0] // 2, pair, 0)


def gather_flux(flux, live):
    vmem = pl.BlockSpec(memory_space=pltpu.VMEM)
    return pl.pallas_call(
        flux_kernel,
        in_specs=[vmem, vmem],
        out_specs=vmem,
        out_shape=jax.ShapeDtypeStruct((flux.shape[0],) + live.shape, jnp.float32),
        compiler_params=pltpu.CompilerParams(vmem_limit_bytes=40 << 20),
    )(flux, live)


def spread_kernel(rows_ref, area_ref, patch_ref, out_ref, hi_s, lo_s):
    freqs, pu, pv = out_ref.shape
    blocks, cap = patch_ref.shape
    group = 8
    out_ref[...] = jnp.zeros_like(out_ref)

    def chunk(t, carry):
        here = pl.ds(group * t, group)
        ids = patch_ref[here, :]
        area = [area_ref[c, here, :] for c in range(3)]
        parts = []
        for f in range(freqs):
            dens = area[0] * rows_ref[3 * f, here, :]
            dens = dens + area[1] * rows_ref[3 * f + 1, here, :]
            dens = dens + area[2] * rows_ref[3 * f + 2, here, :]
            high = dens.astype(jnp.bfloat16).astype(jnp.float32)
            parts.append((high, dens - high))
        for i in range(group):
            lanes = slice(i * cap, (i + 1) * cap)
            row = ids[i : i + 1]
            hi_hit = iota0(pu, cap) == (row >> shift_of(pv))
            hi_s[:, lanes] = hi_hit.astype(jnp.float32).astype(jnp.bfloat16)
            lo_hit = iota0(pv, cap) == (row & (pv - 1))
            for f in range(freqs):
                for p in range(2):
                    lo_s[f, p, :, lanes] = jnp.where(
                        lo_hit, parts[f][p][i : i + 1], 0.0
                    ).astype(jnp.bfloat16)
        nt = (((1,), (1,)), ((), ()))
        for f in range(freqs):
            out_ref[f] += lax.dot_general(
                hi_s[...], lo_s[f, 0], nt, preferred_element_type=jnp.float32
            ) + lax.dot_general(hi_s[...], lo_s[f, 1], nt, preferred_element_type=jnp.float32)
        return carry

    lax.fori_loop(0, blocks // group, chunk, 0)


def spread(rows, area_rows, patch, pu, pv):
    vmem = pl.BlockSpec(memory_space=pltpu.VMEM)
    freqs = rows.shape[0] // 3
    width = 8 * patch.shape[1]
    return pl.pallas_call(
        spread_kernel,
        in_specs=[vmem] * 3,
        out_specs=vmem,
        out_shape=jax.ShapeDtypeStruct((freqs, pu, pv), jnp.float32),
        scratch_shapes=[
            pltpu.VMEM((pu, width), jnp.bfloat16),
            pltpu.VMEM((freqs, 2, pv, width), jnp.bfloat16),
        ],
        compiler_params=pltpu.CompilerParams(vmem_limit_bytes=40 << 20),
    )(rows, area_rows, patch)


def band_matrix(count, half_width):
    row_ids = lax.broadcasted_iota(jnp.int32, (count, count + 2 * half_width), 0)
    col_ids = lax.broadcasted_iota(jnp.int32, (count, count + 2 * half_width), 1)
    return ((col_ids >= row_ids) & (col_ids < row_ids + 2 * half_width)).astype(jnp.float32)


def shards(
    e_field, h_field, j_field, material, material_table, dft_e, dft_h, skin_cell, counts,
    patch_slot, area,
):
    planes, rx = h_field.shape[1:3]
    rows_below = shifted(h_field[1:3, :, -1, :], "gy", 1)
    cols_left = shifted(h_field[0::2, :, :, -1].reshape(2 * planes, rx), "gx", 1)
    blocks, cap = skin_cell.shape[1:]
    patch = patch_slot.reshape(blocks, cap)
    area_rows, live = gather_area(area, patch, skin_cell.reshape(blocks, cap), counts)
    e_next, j_next, dft_e_next, dft_h_next, flux = update_fields(
        h_field, e_field, j_field, material, material_table, rows_below, cols_left, dft_e, dft_h
    )
    arrived = lax.all_to_all(
        gather_flux(flux, live), ("gy", "gx"), split_axis=1, concat_axis=1, tiled=True
    )
    rows_u, cols_v = area.shape[1:]
    point_density = spread(arrived, area_rows, patch, rows_u, cols_v)
    padded = with_halo(point_density, (("gy", 1),), HALF)
    strip_sum = jnp.einsum(
        "ij,fjv->fiv",
        band_matrix(rows_u, HALF),
        padded,
        precision=lax.Precision.HIGHEST,
        preferred_element_type=jnp.float32,
    )
    padded_cols = with_halo(strip_sum, (("gx", 2),), HALF)
    square_sum = jnp.einsum(
        "fuj,ij->fui",
        padded_cols,
        band_matrix(cols_v, HALF),
        precision=lax.Precision.HIGHEST,
        preferred_element_type=jnp.float32,
    )
    avg_density = square_sum / (4.0 * HALF * HALF)
    return (e_next, j_next, dft_e_next, dft_h_next, point_density, avg_density)


def solution(mesh):
    placed = (
        P(None, None, "gy", "gx"),
        P(None, None, "gy", "gx"),
        P(None, None, "gy", "gx"),
        P(None, "gy", "gx"),
        P(),
        P(None, None, None, None, "gy", "gx"),
        P(None, None, None, None, "gy", "gx"),
        P(("gy", "gx"), None, None),
        P(("gy", "gx"), None),
        P(("gy", "gx"), None, None),
        P(None, "gy", "gx"),
    )
    return jax.shard_map(
        shards,
        mesh=mesh,
        in_specs=placed,
        out_specs=(
            P(None, None, "gy", "gx"),
            P(None, None, "gy", "gx"),
            P(None, None, None, None, "gy", "gx"),
            P(None, None, None, None, "gy", "gx"),
            P(None, "gy", "gx"),
            P(None, "gy", "gx"),
        ),
        check_vma=False,
    )
```

time: 433 us -> 87.6 us (0.20)
  the two profiles are of different devices: /device:TPU:21 before, /device:TPU:9 now
where the time goes in v1:
time: 87.6 us; the launch traced here: 87 us
  Pallas kernels  25.3 us (29%)
  waiting for transfers between devices  20.9 us (24%)
  starting transfers between devices  16 us (18%)
  blocking collectives  12.6 us (14%)
  local copies, waits for them, and re-layouts  6.54 us (7%)
  matrix products  4.86 us (6%)
    ppermute x2, waiting for transfers between devices, with_halo(): lax.ppermute(head, axis, [((i + 1) % count, i) for i in range(ends)])  13.3 us
    all_to_all x1, blocking collectives, shards(): lax.all_to_all(gather_flux(flux, live), ('gy', 'gx'), split_axis=1, conca...  12.6 us
    pallas_call x1, Pallas kernels, gather_flux(): pl.pallas_call(flux_kernel, in_specs=[vmem, vmem], out_specs=vmem, out_sh...  8.21 us
    ppermute x2, waiting for transfers between devices, with_halo(): lax.ppermute(tail, axis, [(i, (i + 1) % count) for i in range(ends)])  7.61 us
    ppermute x2, starting transfers between devices, shifted(): lax.ppermute(value, axis, [(source, source + steps) for source in range(l...  7.15 us
    pallas_call x1, Pallas kernels, gather_area(): pl.pallas_call(area_kernel, in_specs=[vmem, vmem, vmem, pl.BlockSpec(memo...  6.78 us
    pallas_call x1, Pallas kernels, spread(): pl.pallas_call(spread_kernel, in_specs=[vmem] * 3, out_specs=vmem, out_sh...  6.56 us
    ppermute x2, starting transfers between devices, with_halo(): lax.ppermute(tail, axis, [(i, (i + 1) % count) for i in range(ends)])  5.38 us
  transfers between devices with their start and end apart: 6, of which 4 were waited for; matrix products, arithmetic and copies ran while one was open for 1% of the time, Pallas kernels for 8%

profile of v1, /device:TPU:9, one launch (start us, length us, event | category | flops | bytes accessed | tf_op | source)
XLA Modules:
  0.0 87.0 jit_solution(14576413898158756559)
XLA Ops:
  0.6 1.2 %slice_reduce_fusion = f32[2,4,64]{2,1,0:T(4,128)S(1)} fusion(f32[3,4,64,128]{3,2,1,0:T(8,128)} %h_ref.1), kind=kLoop, calls=%fused_computation.18 | loop fusion | bytes 4096 | tf_op jit(solution)/shard_map/slice | solution.py:327
  1.9 3.1 %collective-permute-start.1 = (f32[8,64]{1,0:T(8,128)S(1)}, f32[8,64]{1,0:T(8,128)S(1)}, u32[]{:S(2)}, u32[]{:S(2)}) collective-permute-start(f32[8,64]{1,0:T(8,128)S(1)} %bitcast.15), channel_id=1, source_target_pairs={{0,1},{1,2},{2,3},{4,5},{5,6},{6,7},{8,9},{9,10},{10,11},{12,13},{... | collective-permute-start | bytes 6152 | tf_op jit(solution)/shard_map/ppermute | solution.py:21
  5.0 0.8 slice.18
  5.7 4.0 %collective-permute-start = (f32[2,4,128]{2,1,0:T(4,128)S(1)}, f32[2,4,128]{2,1,0:T(4,128)S(1)}, u32[]{:S(2)}, u32[]{:S(2)}) collective-permute-start(f32[2,4,128]{2,1,0:T(4,128)S(1)} %bitcast.16), channel_id=1, source_target_pairs={{0,4},{4,8},{8,12},{12,16},{16,20},{20,24},{24,28},{1,5},{5,9},{9,... | collective-permute-start | bytes 12296 | tf_op jit(solution)/shard_map/ppermute | solution.py:21
  9.8 0.0 copy-start.6
  9.8 0.7 copy-done.6
  10.5 0.0 copy-start.8
  10.5 1.1 %copy-done.8 = f32[3,256,256]{2,1,0:T(8,128)S(1)} copy-done((f32[3,256,256]{2,1,0:T(8,128)S(1)}, f32[3,256,256]{2,1,0:T(8,128)}, u32[]{:S(2)}) %copy-start.8) | copy-done | bytes 786456
  11.6 0.0 copy-start.9
  11.6 0.7 copy-done.9
  12.4 0.0 copy-start.10
  12.4 0.7 copy-done.10
  13.0 0.0 copy-start
  13.0 0.0 copy-start.1
  13.0 0.0 copy-start.2
  13.0 0.0 copy-start.3
  13.0 0.0 copy-start.4
  13.0 0.0 copy-start.5
  13.1 0.0 copy-start.7
  13.1 6.8 %shard_map.155 = (f32[3,32,128]{2,1,0:T(8,128)S(1)}, s32[32,128]{1,0:T(8,128)S(1)}) custom-call(f32[3,256,256]{2,1,0:T(8,128)S(1)} %copy-done.8, s32[32,128]{1,0:T(8,128)S(1)} %bitcast.12, s32[32,128]{1,0:T(8,128)S(1)} %bitcast.14, s32[1,32]{1,0:T(1,128)S(1)} %copy-done.10), custom_call_target="tpu_custom_call" | custom-call | flops 3221225472 | bytes 786432 | tf_op jit(solution)/shard_map/pallas_call | solution.py:203
  19.9 0.0 collective-permute-done.1.cols_ref
  19.9 0.0 collective-permute-done.rows_ref
  19.9 0.0 copy-done
  19.9 0.0 copy-done.1
  19.9 0.0 copy-done.2
  19.9 0.0 copy-done.3
  19.9 0.0 copy-done.4
  19.9 0.0 copy-done.5
  19.9 0.0 copy-done.7
  19.9 3.8 %shard_map.154 = (f32[3,4,64,128]{3,2,1,0:T(8,128)}, f32[3,4,64,128]{3,2,1,0:T(8,128)}, f32[3,2,3,4,64,128]{5,4,3,2,1,0:T(8,128)}, f32[3,2,3,4,64,128]{5,4,3,2,1,0:T(8,128)}, bf16[9,256,256]{2,1,0:T(8,128)(2,1)S(1)}) custom-call(f32[3,4,64,128]{3,2,1,0:T(8,128)S(1)} %copy-done.2, f32[3,4,64,128]{3,2,1,0:T(8,128)S(1)} %copy-done.3, ...), custom_call_target="tpu_custom_call" | custom-call | flops 5898240 | bytes 14680064 | tf_op jit(solution)/shard_map/pallas_call | solution.py:137
  23.7 8.2 %shard_map.156 = f32[9,32,128]{2,1,0:T(8,128)S(1)} custom-call(bf16[9,256,256]{2,1,0:T(8,128)(2,1)S(1)} %get-tuple-element.17.flux_ref, s32[32,128]{1,0:T(8,128)S(1)} %get-tuple-element.18.live_ref), custom_call_target="tpu_custom_call" | custom-call | tf_op jit(solution)/shard_map/pallas_call | solution.py:251
  31.9 0.1 copy.20
  32.0 12.6 %all_to_all.5 = f32[9,32,128]{2,0,1:T(8,128)S(1)} all-to-all(f32[9,32,128]{2,0,1:T(8,128)S(1)} %copy.20), channel_id=1, replica_groups=mesh['gy'=8,'gx'=4] {'gy','gx'}, dimensions={1} | all-to-all | bytes 294912 | tf_op jit(solution)/shard_map/all_to_all | solution.py:334
  44.7 6.6 %shard_map.157 = f32[3,256,256]{2,1,0:T(8,128)} custom-call(f32[9,32,128]{2,1,0:T(8,128)S(1)} %copy.21.rows_ref, f32[3,32,128]{2,1,0:T(8,128)S(1)} %get-tuple-element.19.area_ref, s32[32,128]{1,0:T(8,128)S(1)} %bitcast.13), custom_call_target="tpu_custom_call" | custom-call | tf_op jit(solution)/shard_map/pallas_call | solution.py:302
  51.2 1.1 %fusion.27 = (f32[3,100,256]{2,1,0:T(8,128)S(1)}, f32[3,100,256]{2,1,0:T(8,128)S(1)}) fusion(f32[3,256,256]{2,1,0:T(8,128)} %shard_map.157), kind=kLoop, calls=%fused_computation.25 | loop fusion | bytes 1228800 | tf_op jit(solution)/shard_map/slice | solution.py:29
  52.3 3.1 %collective-permute-start.2 = (f32[3,100,256]{2,1,0:T(8,128)S(1)}, f32[3,100,256]{2,1,0:T(8,128)S(1)}, u32[]{:S(2)}, u32[]{:S(2)}) collective-permute-start(f32[3,100,256]{2,1,0:T(8,128)S(1)} %get-tuple-element.22), channel_id=1, source_target_pairs={{0,4},{4,8},{8,12},{12,16},{16,20},{20,24},{24,28},{1,5},{5,9},{9,... | collective-permute-start | bytes 921608 | tf_op jit(solution)/shard_map/ppermute | solution.py:32
  55.4 2.1 %collective-permute-start.3 = (f32[3,100,256]{2,1,0:T(8,128)S(1)}, f32[3,100,256]{2,1,0:T(8,128)S(1)}, u32[]{:S(2)}, u32[]{:S(2)}) collective-permute-start(f32[3,100,256]{2,1,0:T(8,128)S(1)} %get-tuple-element.23), channel_id=1, source_target_pairs={{4,0},{8,4},{12,8},{16,12},{20,16},{24,20},{28,24},{5,1},{9,5},{13... | collective-permute-start | bytes 921608 | tf_op jit(solution)/shard_map/ppermute | solution.py:34
  57.6 1.7 %collective-permute-done.2 = f32[3,100,256]{2,1,0:T(8,128)S(1)} collective-permute-done((f32[3,100,256]{2,1,0:T(8,128)S(1)}, f32[3,100,256]{2,1,0:T(8,128)S(1)}, u32[]{:S(2)}, u32[]{:S(2)}) %collective-permute-start.2) | collective-permute-done | bytes 307232 | tf_op jit(solution)/shard_map/ppermute | solution.py:32
  59.3 4.4 %collective-permute-done.3 = f32[3,100,256]{2,1,0:T(8,128)S(1)} collective-permute-done((f32[3,100,256]{2,1,0:T(8,128)S(1)}, f32[3,100,256]{2,1,0:T(8,128)S(1)}, u32[]{:S(2)}, u32[]{:S(2)}) %collective-permute-start.3) | collective-permute-done | bytes 307232 | tf_op jit(solution)/shard_map/ppermute | solution.py:34
  63.7 2.6 %fusion.12 = f32[3,256,256]{1,2,0:T(8,128)S(1)} fusion(f32[3,100,256]{2,1,0:T(8,128)S(1)} %collective-permute-done.3, f32[3,256,256]{2,1,0:T(8,128)} %shard_map.157, f32[3,100,256]{2,1,0:T(8,128)S(1)} %collective-permute-done.2, s32[256]{0:T(256)S(1)} %iota_add_fusion), kind=kOutput, calls=%fused_computation.12 | convolution fusion | flops 1076889600 | bytes 2188288 | tf_op jit(solution)/shard_map/ij,fjv->fiv/dot_general | solution.py:340
  66.3 2.3 %collective-permute-start.4 = (f32[3,256,100]{1,2,0:T(8,128)S(1)}, f32[3,256,100]{1,2,0:T(8,128)S(1)}, u32[]{:S(2)}, u32[]{:S(2)}) collective-permute-start(f32[3,256,100]{1,2,0:T(8,128)S(1)} %get-tuple-element.20), channel_id=1, source_target_pairs={{0,1},{1,2},{2,3},{4,5},{5,6},{6,7},{8,9},{9,10},{10,11},{12,13},{... | collective-permute-start | bytes 921608 | tf_op jit(solution)/shard_map/ppermute | solution.py:32
  68.6 1.3 %collective-permute-start.5 = (f32[3,256,100]{1,2,0:T(8,128)S(1)}, f32[3,256,100]{1,2,0:T(8,128)S(1)}, u32[]{:S(2)}, u32[]{:S(2)}) collective-permute-start(f32[3,256,100]{1,2,0:T(8,128)S(1)} %get-tuple-element.21), channel_id=1, source_target_pairs={{1,0},{2,1},{3,2},{5,4},{6,5},{7,6},{9,8},{10,9},{11,10},{13,12},{... | collective-permute-start | bytes 921608 | tf_op jit(solution)/shard_map/ppermute | solution.py:34
  69.9 5.9 %collective-permute-done.4 = f32[3,256,100]{1,2,0:T(8,128)S(1)} collective-permute-done((f32[3,256,100]{1,2,0:T(8,128)S(1)}, f32[3,256,100]{1,2,0:T(8,128)S(1)}, u32[]{:S(2)}, u32[]{:S(2)}) %collective-permute-start.4) | collective-permute-done | bytes 307232 | tf_op jit(solution)/shard_map/ppermute | solution.py:32
  75.8 8.9 %collective-permute-done.5 = f32[3,256,100]{1,2,0:T(8,128)S(1)} collective-permute-done((f32[3,256,100]{1,2,0:T(8,128)S(1)}, f32[3,256,100]{1,2,0:T(8,128)S(1)}, u32[]{:S(2)}, u32[]{:S(2)}) %collective-permute-start.5) | collective-permute-done | bytes 307232 | tf_op jit(solution)/shard_map/ppermute | solution.py:34
  84.7 2.3 %fusion.15 = f32[3,256,256]{2,1,0:T(8,128)} fusion(f32[3,256,100]{1,2,0:T(8,128)S(1)} %collective-permute-done.5, f32[3,256,256]{1,2,0:T(8,128)S(1)} %fusion.12, f32[3,256,100]{1,2,0:T(8,128)S(1)} %collective-permute-done.4, s32[256]{0:T(256)S(1)} %iota_add_fusion), kind=kOutput, calls=%fused_computation.13 | convolution fusion | flops 1077086208 | bytes 2188288 | tf_op jit(solution)/shard_map/fuj,ij->fui/dot_general | solution.py:348
  (3 shorter events, 0.1 us)
Async XLA Ops:
  1.9 18.0 %collective-permute-start.1 = (f32[8,64]{1,0:T(8,128)S(1)}, f32[8,64]{1,0:T(8,128)S(1)}, u32[]{:S(2)}, u32[]{:S(2)}) collective-permute-start(f32[8,64]{1,0:T(8,128)S(1)} %bitcast.15), channel_id=1, source_target_pairs={{0,1},{1,2},{2,3},{4,5},{5,6},{6,7},{8,9},{9,10},{10,11},{12,13},{... | collective-permute-start | bytes 6152 | tf_op jit(solution)/shard_map/ppermute | solution.py:21
  5.7 14.1 %collective-permute-start = (f32[2,4,128]{2,1,0:T(4,128)S(1)}, f32[2,4,128]{2,1,0:T(4,128)S(1)}, u32[]{:S(2)}, u32[]{:S(2)}) collective-permute-start(f32[2,4,128]{2,1,0:T(4,128)S(1)} %bitcast.16), channel_id=1, source_target_pairs={{0,4},{4,8},{8,12},{12,16},{16,20},{20,24},{24,28},{1,5},{5,9},{9,... | collective-permute-start | bytes 12296 | tf_op jit(solution)/shard_map/ppermute | solution.py:21
  9.8 0.7 copy-start.6
  10.5 1.1 %copy-start.8 = (f32[3,256,256]{2,1,0:T(8,128)S(1)}, f32[3,256,256]{2,1,0:T(8,128)}, u32[]{:S(2)}) copy-start(f32[3,256,256]{2,1,0:T(8,128)} %area_ref.1) | copy-start | bytes 2359300
  11.6 0.7 copy-start.9
  12.4 0.7 copy-start.10
  13.0 6.9 %copy-start = (f32[3,2,3,4,64,128]{5,4,3,2,1,0:T(8,128)S(1)}, f32[3,2,3,4,64,128]{5,4,3,2,1,0:T(8,128)}, u32[]{:S(2)}) copy-start(f32[3,2,3,4,64,128]{5,4,3,2,1,0:T(8,128)} %de_ref.1) | copy-start | bytes 7077892
  13.0 6.9 %copy-start.1 = (f32[3,2,3,4,64,128]{5,4,3,2,1,0:T(8,128)S(1)}, f32[3,2,3,4,64,128]{5,4,3,2,1,0:T(8,128)}, u32[]{:S(2)}) copy-start(f32[3,2,3,4,64,128]{5,4,3,2,1,0:T(8,128)} %dh_ref.1) | copy-start | bytes 7077892
  13.0 6.9 %copy-start.2 = (f32[3,4,64,128]{3,2,1,0:T(8,128)S(1)}, f32[3,4,64,128]{3,2,1,0:T(8,128)}, u32[]{:S(2)}) copy-start(f32[3,4,64,128]{3,2,1,0:T(8,128)} %h_ref.1) | copy-start | bytes 1179652
  13.0 6.9 %copy-start.3 = (f32[3,4,64,128]{3,2,1,0:T(8,128)S(1)}, f32[3,4,64,128]{3,2,1,0:T(8,128)}, u32[]{:S(2)}) copy-start(f32[3,4,64,128]{3,2,1,0:T(8,128)} %e_ref.1) | copy-start | bytes 1179652
  13.0 6.9 %copy-start.4 = (f32[3,4,64,128]{3,2,1,0:T(8,128)S(1)}, f32[3,4,64,128]{3,2,1,0:T(8,128)}, u32[]{:S(2)}) copy-start(f32[3,4,64,128]{3,2,1,0:T(8,128)} %j_ref.1) | copy-start | bytes 1179652
  13.0 6.9 %copy-start.5 = (s32[4,64,128]{2,1,0:T(8,128)S(1)}, s32[4,64,128]{2,1,0:T(8,128)}, u32[]{:S(2)}) copy-start(s32[4,64,128]{2,1,0:T(8,128)} %mat_ref.1) | copy-start | bytes 393220
  13.1 6.9 %copy-start.7 = (f32[4,32]{1,0:T(4,128)S(1)}, f32[4,32]{1,0:T(4,128)}, u32[]{:S(2)}) copy-start(f32[4,32]{1,0:T(4,128)} %table_ref.1) | copy-start | bytes 1540
  52.3 7.0 %collective-permute-start.2 = (f32[3,100,256]{2,1,0:T(8,128)S(1)}, f32[3,100,256]{2,1,0:T(8,128)S(1)}, u32[]{:S(2)}, u32[]{:S(2)}) collective-permute-start(f32[3,100,256]{2,1,0:T(8,128)S(1)} %get-tuple-element.22), channel_id=1, source_target_pairs={{0,4},{4,8},{8,12},{12,16},{16,20},{20,24},{24,28},{1,5},{5,9},{9,... | collective-permute-start | bytes 921608 | tf_op jit(solution)/shard_map/ppermute | solution.py:32
  55.4 8.3 %collective-permute-start.3 = (f32[3,100,256]{2,1,0:T(8,128)S(1)}, f32[3,100,256]{2,1,0:T(8,128)S(1)}, u32[]{:S(2)}, u32[]{:S(2)}) collective-permute-start(f32[3,100,256]{2,1,0:T(8,128)S(1)} %get-tuple-element.23), channel_id=1, source_target_pairs={{4,0},{8,4},{12,8},{16,12},{20,16},{24,20},{28,24},{5,1},{9,5},{13... | collective-permute-start | bytes 921608 | tf_op jit(solution)/shard_map/ppermute | solution.py:34
  66.3 9.5 %collective-permute-start.4 = (f32[3,256,100]{1,2,0:T(8,128)S(1)}, f32[3,256,100]{1,2,0:T(8,128)S(1)}, u32[]{:S(2)}, u32[]{:S(2)}) collective-permute-start(f32[3,256,100]{1,2,0:T(8,128)S(1)} %get-tuple-element.20), channel_id=1, source_target_pairs={{0,1},{1,2},{2,3},{4,5},{5,6},{6,7},{8,9},{9,10},{10,11},{12,13},{... | collective-permute-start | bytes 921608 | tf_op jit(solution)/shard_map/ppermute | solution.py:32
  68.6 16.1 %collective-permute-start.5 = (f32[3,256,100]{1,2,0:T(8,128)S(1)}, f32[3,256,100]{1,2,0:T(8,128)S(1)}, u32[]{:S(2)}, u32[]{:S(2)}) collective-permute-start(f32[3,256,100]{1,2,0:T(8,128)S(1)} %get-tuple-element.21), channel_id=1, source_target_pairs={{1,0},{2,1},{3,2},{5,4},{6,5},{7,6},{9,8},{10,9},{11,10},{13,12},{... | collective-permute-start | bytes 921608 | tf_op jit(solution)/shard_map/ppermute | solution.py:34

commit v2 on v1

v2 whole, which is shorter than its diff:
```python
import math

import jax
import jax.numpy as jnp
from jax import lax
from jax.experimental import pallas as pl
from jax.experimental.pallas import tpu as pltpu
from jax.sharding import PartitionSpec as P

STEP = 1000
HALF = 100


FREQ_LIST = (28000000000.0, 39000000000.0, 60000000000.0)
TIME_STEP = 1.9e-13


MESH = pl.DeviceIdType.MESH


def phase_list(offset):
    return [2.0 * math.pi * freq_hz * (STEP + offset) * TIME_STEP for freq_hz in FREQ_LIST]


def shift_of(size):
    return size.bit_length() - 1


def iota0(rows, cols):
    return lax.broadcasted_iota(jnp.int32, (rows, cols), 0)


def split_two(values):
    first = values.astype(jnp.bfloat16)
    return first, (values - first.astype(jnp.float32)).astype(jnp.bfloat16)


def field_kernel(
    h_ref, e_ref, j_ref, mat_ref, table_ref, rows_ref, cols_ref, de_ref, dh_ref,
    en_ref, jn_ref, den_ref, dhn_ref, flux_ref, table_s,
):
    step = pl.program_id(0)
    per, rx, cy = mat_ref.shape
    planes = h_ref.shape[1]
    freqs = de_ref.shape[0]
    table_s[...] = jnp.zeros_like(table_s)
    table_s[0:4, 0 : table_ref.shape[1]] = table_ref[...]
    first_row = iota0(rx, cy) == 0
    first_col = lax.broadcasted_iota(jnp.int32, (rx, cy), 1) == 0
    cos_e = [math.cos(a) for a in phase_list(0.0)]
    sin_e = [-math.sin(a) for a in phase_list(0.0)]
    cos_h = [math.cos(a) for a in phase_list(0.5)]
    sin_h = [-math.sin(a) for a in phase_list(0.5)]

    def row_below(value, comp, z):
        edge = jnp.broadcast_to(rows_ref[pl.ds(comp * planes + z, 1), :], (rx, cy))
        return jnp.where(first_row, edge, pltpu.roll(value, 1, 0))

    def col_below(value, comp, z):
        line = cols_ref[pl.ds(comp * planes + z, 1), :]
        edge = jnp.broadcast_to(line, (cy, cy)).T[:rx]
        return jnp.where(first_col, edge, pltpu.roll(value, 1, 1))

    for k in range(per):
        z = step * per + k
        below = jnp.maximum(z - 1, 0)
        keep = jnp.where(z > 0, 1.0, 0.0)
        hx, hy, hz = (h_ref[c, z] for c in range(3))
        curl = (
            (hz - col_below(hz, 1, z)) - (hy - h_ref[1, below] * keep),
            (hx - h_ref[0, below] * keep) - (hz - row_below(hz, 1, z)),
            (hy - row_below(hy, 0, z)) - (hx - col_below(hx, 0, z)),
        )
        kinds = mat_ref[k]
        coeffs = [
            jnp.take_along_axis(
                jnp.broadcast_to(table_s[r : r + 1, :], (rx, cy)), kinds, axis=1,
                mode="promise_in_bounds",
            )
            for r in range(4)
        ]
        en = []
        for c in range(3):
            e_old, j_old = e_ref[c, k], j_ref[c, k]
            e_new = coeffs[0] * e_old + coeffs[1] * (curl[c] - j_old)
            en_ref[c, k] = e_new
            jn_ref[c, k] = coeffs[2] * j_old + coeffs[3] * (e_new - e_old)
            en.append(e_new)
        h_now = (hx, hy, hz)
        for f in range(freqs):
            spectra = []
            for part in range(2):
                e_scale = (cos_e, sin_e)[part][f]
                h_scale = (cos_h, sin_h)[part][f]
                e_part = [de_ref[f, part, c, k] + en[c] * e_scale for c in range(3)]
                h_part = [dh_ref[f, part, c, k] + h_now[c] * h_scale for c in range(3)]
                for c in range(3):
                    den_ref[f, part, c, k] = e_part[c]
                    dhn_ref[f, part, c, k] = h_part[c]
                spectra.append((e_part, h_part))
            for c in range(3):
                a, b = (c + 1) % 3, (c + 2) % 3
                real, imag = [ep[a] * hp[b] - ep[b] * hp[a] for ep, hp in spectra]
                high, low = split_two(0.5 * (real + imag))
                flux_ref[f * 3 + c, k * rx : (k + 1) * rx, 0:cy] = high
                flux_ref[f * 3 + c, k * rx : (k + 1) * rx, cy : 2 * cy] = low


def update_fields(h, e, j, material, table, rows, cols, dft_e, dft_h):
    _, planes, rx, cy = h.shape
    freqs = dft_e.shape[0]
    per = 2 if planes % 2 == 0 else 1
    field_block = pl.BlockSpec((3, per, rx, cy), lambda s: (0, s, 0, 0))
    dft_block = pl.BlockSpec((freqs, 2, 3, per, rx, cy), lambda s: (0, 0, 0, s, 0, 0))
    return pl.pallas_call(
        field_kernel,
        grid=(planes // per,),
        in_specs=[
            pl.BlockSpec(h.shape, lambda s: (0, 0, 0, 0)),
            field_block,
            field_block,
            pl.BlockSpec((per, rx, cy), lambda s: (s, 0, 0)),
            pl.BlockSpec(table.shape, lambda s: (0, 0)),
            pl.BlockSpec(rows.shape, lambda s: (0, 0)),
            pl.BlockSpec(cols.shape, lambda s: (0, 0)),
            dft_block,
            dft_block,
        ],
        out_specs=[
            field_block, field_block, dft_block, dft_block,
            pl.BlockSpec((3 * freqs, per * rx, 2 * cy), lambda s: (0, s, 0)),
        ],
        out_shape=[
            jax.ShapeDtypeStruct(e.shape, jnp.float32),
            jax.ShapeDtypeStruct(j.shape, jnp.float32),
            jax.ShapeDtypeStruct(dft_e.shape, jnp.float32),
            jax.ShapeDtypeStruct(dft_h.shape, jnp.float32),
            jax.ShapeDtypeStruct((3 * freqs, planes * rx, 2 * cy), jnp.bfloat16),
        ],
        scratch_shapes=[pltpu.VMEM((8, cy), jnp.float32)],
        compiler_params=pltpu.CompilerParams(vmem_limit_bytes=40 << 20),
        cost_estimate=pl.CostEstimate(flops=10 * dft_e.size, bytes_accessed=14 << 20, transcendentals=0),
    )(h, e, j, material, table, rows, cols, dft_e, dft_h)


def signal(sem, where):
    pl.semaphore_signal(sem, inc=1, device_id=where, device_id_type=MESH)


def remote(src, dst, send_sem, recv_sem, where):
    return pltpu.make_async_remote_copy(
        src_ref=src, dst_ref=dst, send_sem=send_sem, recv_sem=recv_sem,
        device_id=where, device_id_type=MESH,
    )


def area_kernel(
    h_any, area_any, patch_ref, skin_ref, counts_ref,
    out_ref, live_ref, rows_ref, cols_ref,
    h_s, area_s, split_s, row_edge, col_edge, load_sem, send_sem, recv_sem,
):
    comps, pu, pv = area_s.shape
    blocks, cap = patch_ref.shape
    _, planes, rx, cy = h_s.shape
    axes = ("gy", "gx")
    place = [lax.axis_index(axis) for axis in axes]
    count = [lax.axis_size(axis) for axis in axes]
    h_load = pltpu.make_async_copy(h_any, h_s, load_sem.at[0])
    area_load = pltpu.make_async_copy(area_any, area_s, load_sem.at[1])
    h_load.start()
    area_load.start()
    barrier = pltpu.get_barrier_semaphore()
    for axis, at in zip(axes, place):

        @pl.when(at > 0)
        def _():
            signal(barrier, {axis: at - 1})

    h_load.wait()
    col_edge[...] = jnp.zeros_like(col_edge)
    for k in range(2):
        for z in range(planes):
            line = k * planes + z
            row_edge[line : line + 1, :] = h_s[1 + k, z, rx - 1 : rx, :]
            col_edge[line : line + 1, 0:rx] = h_s[2 * k, z].T[cy - 1 : cy, :]
    edges = (row_edge, col_edge)
    landing = (rows_ref, cols_ref)
    copies = [
        remote(edges[i], landing[i], send_sem.at[i], recv_sem.at[i], {axes[i]: place[i] + 1})
        for i in range(2)
    ]
    peers = sum(jnp.where(at < size - 1, 1, 0) for at, size in zip(place, count))

    @pl.when(peers > 0)
    def _():
        pl.semaphore_wait(barrier, peers)

    for i in range(2):

        @pl.when(place[i] < count[i] - 1)
        def _():
            copies[i].start()

        @pl.when(place[i] == 0)
        def _():
            landing[i][...] = jnp.zeros_like(landing[i])

    area_load.wait()
    for c in range(comps):
        high, low = split_two(area_s[c])
        split_s[c, :, 0:pv] = high
        split_s[c, :, pv : 2 * pv] = low
    slots = lax.broadcasted_iota(jnp.int32, (1, cap), 1)

    def one_group(t, carry):
        for q in range(4):
            first = 8 * t + 2 * q
            ids = jnp.concatenate([patch_ref[pl.ds(first + i, 1), :] for i in range(2)], 1)
            low = (iota0(pv, 2 * cap) == (ids & (pv - 1))).astype(jnp.float32)
            low = low.astype(jnp.bfloat16)
            both = jnp.concatenate([low, low], 0)
            hit = iota0(pu, 2 * cap) == (ids >> shift_of(pv))
            for c in range(comps):
                rows = jnp.dot(split_s[c], both, preferred_element_type=jnp.float32)
                value = jnp.sum(jnp.where(hit, rows, 0.0), axis=0, keepdims=True)
                for i in range(2):
                    out_ref[c, pl.ds(first + i, 1), :] = value[:, i * cap : (i + 1) * cap]
        here = pl.ds(pl.multiple_of(8 * t, 8), 8)
        live_ref[here, :] = jnp.where(slots < counts_ref[here, :], skin_ref[here, :], -1)
        return carry

    lax.fori_loop(0, blocks // 8, one_group, 0)
    for i in range(2):

        @pl.when(place[i] < count[i] - 1)
        def _():
            copies[i].wait_send()

        @pl.when(place[i] > 0)
        def _():
            copies[i].wait_recv()


def gather_area(h, area, patch, skin, counts):
    vmem = pl.BlockSpec(memory_space=pltpu.VMEM)
    blocks, cap = patch.shape
    _, planes, rx, cy = h.shape
    edge = (2 * planes, cy)
    return pl.pallas_call(
        area_kernel,
        in_specs=[pl.BlockSpec(memory_space=pl.ANY)] * 2 + [vmem] * 3,
        out_specs=[vmem] * 4,
        out_shape=[
            jax.ShapeDtypeStruct((area.shape[0],) + patch.shape, jnp.float32),
            jax.ShapeDtypeStruct(skin.shape, jnp.int32),
            jax.ShapeDtypeStruct(edge, jnp.float32),
            jax.ShapeDtypeStruct(edge, jnp.float32),
        ],
        scratch_shapes=[
            pltpu.VMEM(h.shape, jnp.float32),
            pltpu.VMEM(area.shape, jnp.float32),
            pltpu.VMEM((area.shape[0], area.shape[1], 2 * area.shape[2]), jnp.bfloat16),
            pltpu.VMEM(edge, jnp.float32),
            pltpu.VMEM(edge, jnp.float32),
            pltpu.SemaphoreType.DMA((2,)),
            pltpu.SemaphoreType.DMA((2,)),
            pltpu.SemaphoreType.DMA((2,)),
        ],
        compiler_params=pltpu.CompilerParams(
            vmem_limit_bytes=40 << 20, collective_id=0, has_side_effects=True
        ),
    )(h, area, patch, skin, counts)


def flux_pair(flux_ref, live_ref, t):
    rows, hi_count, two_lo = flux_ref.shape
    lo_count = two_lo // 2
    ids = jnp.concatenate([live_ref[pl.ds(2 * t + i, 1), :] for i in range(2)], 1)
    width = ids.shape[1]
    low = (iota0(lo_count, width) == (ids & (lo_count - 1))).astype(jnp.float32)
    low = low.astype(jnp.bfloat16)
    both = jnp.concatenate([low, low], 0)
    hit = iota0(hi_count, width) == (ids >> shift_of(lo_count))
    picked = []
    for r in range(rows):
        part = jnp.dot(flux_ref[r], both, preferred_element_type=jnp.float32)
        picked.append(jnp.sum(jnp.where(hit, part, 0.0), axis=0, keepdims=True))
    return picked


def flux_kernel(flux_ref, live_ref, out_ref, pack_s, send_sem, recv_sem):
    blocks, cap = live_ref.shape
    n_gx = lax.axis_size("gx")
    me = lax.axis_index("gy") * n_gx + lax.axis_index("gx")
    groups = blocks // 8
    barrier = pltpu.get_barrier_semaphore()

    def greet(k, carry):
        d = (me + k) % blocks
        signal(barrier, (d // n_gx, d % n_gx))
        return carry

    lax.fori_loop(1, blocks, greet, 0)

    def gather_group(step):
        group = (me // 8 + step) % groups
        for q in range(4):
            picked = flux_pair(flux_ref, live_ref, group * 4 + q)
            for r, value in enumerate(picked):
                for i in range(2):
                    pack_s[group * 8 + 2 * q + i, r : r + 1, :] = value[:, i * cap : (i + 1) * cap]
        return group

    def copy_to(d):
        return remote(
            pack_s.at[d], out_ref.at[me], send_sem.at[d], recv_sem.at[me],
            (d // n_gx, d % n_gx),
        )

    def send_group(group):
        def send_one(i, carry):
            d = group * 8 + i

            @pl.when(d != me)
            def _():
                copy_to(d).start()

            return carry

        lax.fori_loop(0, 8, send_one, 0)

    own = gather_group(0)
    out_ref[me] = pack_s[me]
    pl.semaphore_wait(barrier, blocks - 1)
    send_group(own)

    def one_step(step, carry):
        send_group(gather_group(step))
        return carry

    lax.fori_loop(1, groups, one_step, 0)

    def finish(k, carry):
        d = (me + k) % blocks
        copy_to(d).wait_send()
        remote(
            pack_s.at[d], out_ref.at[d], send_sem.at[d], recv_sem.at[d],
            (d // n_gx, d % n_gx),
        ).wait_recv()
        return carry

    lax.fori_loop(1, blocks, finish, 0)


def exchange_flux(flux, live):
    vmem = pl.BlockSpec(memory_space=pltpu.VMEM)
    blocks, cap = live.shape
    shape = (blocks, flux.shape[0], cap)
    return pl.pallas_call(
        flux_kernel,
        in_specs=[vmem, vmem],
        out_specs=vmem,
        out_shape=jax.ShapeDtypeStruct(shape, jnp.float32),
        scratch_shapes=[
            pltpu.VMEM(shape, jnp.float32),
            pltpu.SemaphoreType.DMA((blocks,)),
            pltpu.SemaphoreType.DMA((blocks,)),
        ],
        compiler_params=pltpu.CompilerParams(
            vmem_limit_bytes=40 << 20, collective_id=1, has_side_effects=True
        ),
    )(flux, live)


NT = (((1,), (1,)), ((), ()))
REACH = 104
PAD = 128


def band_kernel(
    rows_ref, area_ref, patch_ref, point_ref, avg_ref,
    dens_s, side_dens, side_patch, hi_own, hi_side, strip_s,
    send_sem, recv_sem, u_send, u_recv,
):
    freqs, pu, pv = point_ref.shape
    blocks, cap = patch_ref.shape
    gy, gx = lax.axis_index("gy"), lax.axis_index("gx")
    n_gy, n_gx = lax.axis_size("gy"), lax.axis_size("gx")
    sides = [("gx", gx > 0, gx - 1), ("gx", gx < n_gx - 1, gx + 1)]
    ends = [("gy", gy > 0, gy - 1), ("gy", gy < n_gy - 1, gy + 1)]
    barrier = pltpu.get_barrier_semaphore()
    for axis, there, at in sides + ends:

        @pl.when(there)
        def _():
            signal(barrier, {axis: at})

    for f in range(freqs):
        dens = area_ref[0] * rows_ref[:, 3 * f, :]
        dens = dens + area_ref[1] * rows_ref[:, 3 * f + 1, :]
        dens_s[f] = dens + area_ref[2] * rows_ref[:, 3 * f + 2, :]
    pl.semaphore_wait(barrier, sum(jnp.where(there, 1, 0) for _, there, _ in sides + ends))
    side_copies = []
    for i, (axis, there, at) in enumerate(sides):
        copies = [
            remote(dens_s, side_dens.at[1 - i], send_sem.at[i, 0], recv_sem.at[1 - i, 0], {axis: at}),
            remote(patch_ref, side_patch.at[1 - i], send_sem.at[i, 1], recv_sem.at[1 - i, 1], {axis: at}),
        ]
        arrivals = [
            remote(dens_s, side_dens.at[i], send_sem.at[i, 0], recv_sem.at[i, 0], {axis: at}),
            remote(patch_ref, side_patch.at[i], send_sem.at[i, 1], recv_sem.at[i, 1], {axis: at}),
        ]
        side_copies.append((there, copies, arrivals))

        @pl.when(there)
        def _():
            for copy in copies:
                copy.start()

        @pl.when(jnp.logical_not(there))
        def _():
            side_dens[i] = jnp.zeros_like(side_dens.at[i])
            side_patch[i] = jnp.zeros_like(side_patch.at[i])

    strip_s[:, 0 : PAD - REACH, :] = jnp.zeros((freqs, PAD - REACH, pv), jnp.float32)
    strip_s[:, pu + PAD + REACH :, :] = jnp.zeros((freqs, PAD - REACH, pv), jnp.float32)
    landing = [pl.ds(PAD - REACH, REACH), pl.ds(PAD + pu, REACH)]
    leaving = [pl.ds(PAD, REACH), pl.ds(PAD + pu - REACH, REACH)]
    for i, (axis, there, at) in enumerate(ends):

        @pl.when(jnp.logical_not(there))
        def _():
            strip_s[:, landing[i], :] = jnp.zeros((freqs, REACH, pv), jnp.float32)

    group = 32 if blocks % 32 == 0 else blocks
    groups = blocks // group

    def rows_of(ids, i):
        return ids[i : i + 1]

    def hi_part(ids, size):
        pieces = [
            (iota0(size, cap) == (rows_of(ids, i) >> shift_of(pv))).astype(jnp.float32)
            for i in range(group)
        ]
        return jnp.concatenate(pieces, 1).astype(jnp.bfloat16)

    def own_step(f, t):
        here = pl.ds(pl.multiple_of(t * group, 8), group)
        ids = patch_ref[here, :]
        if f == 0:
            hi = hi_part(ids, pu)
            hi_own[t] = hi
        else:
            hi = hi_own[t]
        dens = dens_s[f, here, :]
        first = dens.astype(jnp.bfloat16).astype(jnp.float32)
        out = None
        hits = [iota0(pv, cap) == (rows_of(ids, i) & (pv - 1)) for i in range(group)]
        for part in (first, dens - first):
            spread = jnp.concatenate(
                [
                    jnp.where(hits[i], rows_of(part, i), 0.0).astype(jnp.bfloat16)
                    for i in range(group)
                ],
                1,
            )
            one = lax.dot_general(hi, spread, NT, preferred_element_type=jnp.float32)
            out = one if out is None else out + one
        return out

    def own(f):
        point_ref[f] = own_step(f, 0)

        def more(t, carry):
            point_ref[f] += own_step(f, t)
            return carry

        if groups > 1:
            lax.fori_loop(1, groups, more, 0)

    half = pv // 2

    def side_step(f, i, t):
        here = pl.ds(pl.multiple_of(t * group, 8), group)
        ids = side_patch[i, here, :]
        if f == 0:
            hi = hi_part(ids, pu)
            hi_side[i, t] = hi
        else:
            hi = hi_side[i, t]
        dens = side_dens[i, f, here, :]
        first = dens.astype(jnp.bfloat16).astype(jnp.float32)
        rest = dens - first
        pieces = []
        for s in range(group):
            cell = rows_of(ids, s) & (pv - 1)
            if i == 0:
                within = cell >= iota0(half, cap) + (pv - HALF)
            else:
                within = cell <= iota0(half, cap) + (half - 1 - pv + HALF)
            pieces.append(
                jnp.concatenate(
                    [jnp.where(within, rows_of(part, s), 0.0) for part in (first, rest)], 0
                ).astype(jnp.bfloat16)
            )
        out = lax.dot_general(
            hi, jnp.concatenate(pieces, 1), NT, preferred_element_type=jnp.float32
        )
        return out[:, :half] + out[:, half:]

    rows_at = pl.ds(PAD, pu)

    def strip(f):
        k, v = iota0(pv, pv), lax.broadcasted_iota(jnp.int32, (pv, pv), 1)
        band = ((k >= v - HALF) & (k < v + HALF)).astype(jnp.float32).astype(jnp.bfloat16)
        high, low = split_two(point_ref[f])
        mid = jnp.dot(high, band, preferred_element_type=jnp.float32)
        mid = mid + jnp.dot(low, band, preferred_element_type=jnp.float32)
        strip_s[f, rows_at, 0:half] = mid[:, :half] + side_step(f, 0, 0)
        strip_s[f, rows_at, half:pv] = mid[:, half:] + side_step(f, 1, 0)

        def more(t, carry):
            strip_s[f, rows_at, 0:half] += side_step(f, 0, t)
            strip_s[f, rows_at, half:pv] += side_step(f, 1, t)
            return carry

        if groups > 1:
            lax.fori_loop(1, groups, more, 0)

    def end_copy(f, i, arrival):
        axis, there, at = ends[i]
        lands = i if arrival else 1 - i
        return remote(
            strip_s.at[f, leaving[i]], strip_s.at[f, landing[lands]],
            u_send.at[f, i], u_recv.at[f, lands], {axis: at},
        )

    def send_ends(f):
        for i, (axis, there, at) in enumerate(ends):

            @pl.when(there)
            def _():
                end_copy(f, i, False).start()

    def average(f):
        for i, (axis, there, at) in enumerate(ends):

            @pl.when(there)
            def _():
                end_copy(f, i, True).wait_recv()

        u = iota0(pu, pu + 2 * PAD)
        g = lax.broadcasted_iota(jnp.int32, (pu, pu + 2 * PAD), 1) - PAD
        band = ((g >= u - HALF) & (g < u + HALF)).astype(jnp.float32).astype(jnp.bfloat16)
        high, low = split_two(strip_s[f])
        total = jnp.dot(band, high, preferred_element_type=jnp.float32)
        total = total + jnp.dot(band, low, preferred_element_type=jnp.float32)
        avg_ref[f] = total * (1.0 / (4.0 * HALF * HALF))

    own(0)
    own(1)
    for there, copies, arrivals in side_copies:

        @pl.when(there)
        def _():
            for copy in arrivals:
                copy.wait_recv()

    strip(0)
    send_ends(0)
    own(2)
    strip(1)
    send_ends(1)
    strip(2)
    send_ends(2)
    for f in range(freqs):
        average(f)
    for there, copies, arrivals in side_copies:

        @pl.when(there)
        def _():
            for copy in copies:
                copy.wait_send()

    for f in range(freqs):
        for i, (axis, there, at) in enumerate(ends):

            @pl.when(there)
            def _():
                end_copy(f, i, False).wait_send()


def surface(rows, area_rows, patch, pu, pv):
    vmem = pl.BlockSpec(memory_space=pltpu.VMEM)
    blocks, cap = patch.shape
    freqs = rows.shape[1] // 3
    group = 32 if blocks % 32 == 0 else blocks
    out = jax.ShapeDtypeStruct((freqs, pu, pv), jnp.float32)
    return pl.pallas_call(
        band_kernel,
        in_specs=[vmem] * 3,
        out_specs=[vmem] * 2,
        out_shape=[out, out],
        scratch_shapes=[
            pltpu.VMEM((freqs, blocks, cap), jnp.float32),
            pltpu.VMEM((2, freqs, blocks, cap), jnp.float32),
            pltpu.VMEM((2, blocks, cap), jnp.int32),
            pltpu.VMEM((blocks // group, pu, group * cap), jnp.bfloat16),
            pltpu.VMEM((2, blocks // group, pu, group * cap), jnp.bfloat16),
            pltpu.VMEM((freqs, pu + 2 * PAD, pv), jnp.float32),
            pltpu.SemaphoreType.DMA((2, 2)),
            pltpu.SemaphoreType.DMA((2, 2)),
            pltpu.SemaphoreType.DMA((freqs, 2)),
            pltpu.SemaphoreType.DMA((freqs, 2)),
        ],
        compiler_params=pltpu.CompilerParams(
            vmem_limit_bytes=52 << 20, collective_id=2, has_side_effects=True
        ),
    )(rows, area_rows, patch)


def shards(
    e_field, h_field, j_field, material, material_table, dft_e, dft_h, skin_cell, counts,
    patch_slot, area,
):
    blocks, cap = skin_cell.shape[1:]
    patch = patch_slot.reshape(blocks, cap)
    area_rows, live, rows_below, cols_left = gather_area(
        h_field, area, patch, skin_cell.reshape(blocks, cap), counts.reshape(blocks, 1)
    )
    e_next, j_next, dft_e_next, dft_h_next, flux = update_fields(
        h_field, e_field, j_field, material, material_table, rows_below, cols_left, dft_e, dft_h
    )
    arrived = exchange_flux(flux, live)
    point_density, avg_density = surface(arrived, area_rows, patch, area.shape[1], area.shape[2])
    return (e_next, j_next, dft_e_next, dft_h_next, point_density, avg_density)


def solution(mesh):
    placed = (
        P(None, None, "gy", "gx"),
        P(None, None, "gy", "gx"),
        P(None, None, "gy", "gx"),
        P(None, "gy", "gx"),
        P(),
        P(None, None, None, None, "gy", "gx"),
        P(None, None, None, None, "gy", "gx"),
        P(("gy", "gx"), None, None),
        P(("gy", "gx"), None),
        P(("gy", "gx"), None, None),
        P(None, "gy", "gx"),
    )
    return jax.shard_map(
        shards,
        mesh=mesh,
        in_specs=placed,
        out_specs=(
            P(None, None, "gy", "gx"),
            P(None, None, "gy", "gx"),
            P(None, None, None, None, "gy", "gx"),
            P(None, None, None, None, "gy", "gx"),
            P(None, "gy", "gx"),
            P(None, "gy", "gx"),
        ),
        check_vma=False,
    )
```

time: 87.6 us -> 54.2 us (0.62)
  the two profiles are of different devices: /device:TPU:9 before, /device:TPU:21 now
where the time goes in v2:
time: 54.2 us; the launch traced here: 53.6 us
  Pallas kernels  40 us (74%)
  local copies, waits for them, and re-layouts  13 us (24%)
  between operations  0.68 us (1%)
    pallas_call x1, Pallas kernels, surface(): pl.pallas_call(band_kernel, in_specs=[vmem] * 3, out_specs=[vmem] * 2, ou...  18.1 us
    unnamed x24, local copies, waits for them, and re-layouts  12.2 us
    pallas_call x1, Pallas kernels, exchange_flux(): pl.pallas_call(flux_kernel, in_specs=[vmem, vmem], out_specs=vmem, out_sh...  11.7 us
    pallas_call x1, Pallas kernels, gather_area(): pl.pallas_call(area_kernel, in_specs=[pl.BlockSpec(memory_space=pl.ANY)]...  6.4 us
    pallas_call x1, Pallas kernels, update_fields(): pl.pallas_call(field_kernel, grid=(planes // per,), in_specs=[pl.BlockSpe...  3.71 us

profile of v2, /device:TPU:21, one launch (start us, length us, event | category | flops | bytes accessed | tf_op | source)
XLA Modules:
  0.0 53.6 jit_solution(17239105022209302643)
XLA Ops:
  0.6 0.7 %copy.17.counts_ref = s32[32,1]{1,0:T(8,128)S(1)} copy(s32[32,1]{0,1:T(1,128)} %bitcast.6) | data formatting | bytes 256 | tf_op jit(solution)/shard_map/reshape | solution.py:630
  1.4 0.0 copy-start.2
  1.4 1.0 %copy-done.2 = f32[3,4,64,128]{3,2,1,0:T(8,128)S(1)} copy-done((f32[3,4,64,128]{3,2,1,0:T(8,128)S(1)}, f32[3,4,64,128]{3,2,1,0:T(8,128)}, u32[]{:S(2)}) %copy-start.2) | copy-done | bytes 393240
  2.4 0.0 copy-start.3
  2.4 1.1 %copy-done.3 = f32[3,256,256]{2,1,0:T(8,128)S(1)} copy-done((f32[3,256,256]{2,1,0:T(8,128)S(1)}, f32[3,256,256]{2,1,0:T(8,128)}, u32[]{:S(2)}) %copy-start.3) | copy-done | bytes 786456
  3.5 0.0 copy-start.7
  3.5 0.7 %copy-done.7 = s32[1,32,128]{2,1,0:T(8,128)S(1)} copy-done((s32[1,32,128]{2,1,0:T(8,128)S(1)}, s32[1,32,128]{2,1,0:T(8,128)}, u32[]{:S(2)}) %copy-start.7) | copy-done | bytes 16408
  4.2 0.0 copy-start.9
  4.2 0.7 %copy-done.9 = s32[1,32,128]{2,1,0:T(8,128)S(1)} copy-done((s32[1,32,128]{2,1,0:T(8,128)S(1)}, s32[1,32,128]{2,1,0:T(8,128)}, u32[]{:S(2)}) %copy-start.9) | copy-done | bytes 16408
  4.9 6.4 %shard_map.154 = (f32[3,32,128]{2,1,0:T(8,128)S(1)}, s32[32,128]{1,0:T(8,128)S(1)}, f32[8,128]{1,0:T(8,128)S(1)}, f32[8,128]{1,0:T(8,128)S(1)}) custom-call(f32[3,4,64,128]{3,2,1,0:T(8,128)S(1)} %copy-done.2, f32[3,256,256]{2,1,0:T(8,128)S(1)} %copy-done.3, s32[32,128]{1,0:T(8,128)S(1)} %bitcast.3, s32[32,128]{1,0:T(8,128)S(1)} %bitcast.5, ...), custom_call_target="tpu_custom_call" | custom-call | tf_op jit(solution)/shard_map/pallas_call | solution.py:249
  11.3 0.0 copy-start
  11.4 1.7 %copy-done = f32[3,2,3,4,64,128]{5,4,3,2,1,0:T(8,128)S(1)} copy-done((f32[3,2,3,4,64,128]{5,4,3,2,1,0:T(8,128)S(1)}, f32[3,2,3,4,64,128]{5,4,3,2,1,0:T(8,128)}, u32[]{:S(2)}) %copy-start) | copy-done | bytes 2359320
  13.0 0.0 copy-start.1
  13.0 1.7 %copy-done.1 = f32[3,2,3,4,64,128]{5,4,3,2,1,0:T(8,128)S(1)} copy-done((f32[3,2,3,4,64,128]{5,4,3,2,1,0:T(8,128)S(1)}, f32[3,2,3,4,64,128]{5,4,3,2,1,0:T(8,128)}, u32[]{:S(2)}) %copy-start.1) | copy-done | bytes 2359320
  14.7 0.0 copy-start.4
  14.7 1.0 %copy-done.4 = f32[3,4,64,128]{3,2,1,0:T(8,128)S(1)} copy-done((f32[3,4,64,128]{3,2,1,0:T(8,128)S(1)}, f32[3,4,64,128]{3,2,1,0:T(8,128)}, u32[]{:S(2)}) %copy-start.4) | copy-done | bytes 393240
  15.7 0.0 copy-start.5
  15.7 1.0 %copy-done.5 = f32[3,4,64,128]{3,2,1,0:T(8,128)S(1)} copy-done((f32[3,4,64,128]{3,2,1,0:T(8,128)S(1)}, f32[3,4,64,128]{3,2,1,0:T(8,128)}, u32[]{:S(2)}) %copy-start.5) | copy-done | bytes 393240
  16.7 0.0 copy-start.6
  16.7 0.9 %copy-done.6 = s32[4,64,128]{2,1,0:T(8,128)S(1)} copy-done((s32[4,64,128]{2,1,0:T(8,128)S(1)}, s32[4,64,128]{2,1,0:T(8,128)}, u32[]{:S(2)}) %copy-start.6) | copy-done | bytes 131096
  17.6 0.0 copy-start.10
  17.6 0.7 %copy-done.10 = f32[4,32]{1,0:T(4,128)S(1)} copy-done((f32[4,32]{1,0:T(4,128)S(1)}, f32[4,32]{1,0:T(4,128)}, u32[]{:S(2)}) %copy-start.10) | copy-done | bytes 536
  18.3 0.0 copy-start.8
  18.3 3.7 %shard_map.155 = (f32[3,4,64,128]{3,2,1,0:T(8,128)}, f32[3,4,64,128]{3,2,1,0:T(8,128)}, f32[3,2,3,4,64,128]{5,4,3,2,1,0:T(8,128)}, f32[3,2,3,4,64,128]{5,4,3,2,1,0:T(8,128)}, bf16[9,256,256]{2,1,0:T(8,128)(2,1)S(1)}) custom-call(f32[3,4,64,128]{3,2,1,0:T(8,128)S(1)} %copy-done.2, f32[3,4,64,128]{3,2,1,0:T(8,128)S(1)} %copy-done.4, ...), custom_call_target="tpu_custom_call" | custom-call | flops 5898240 | bytes 14680064 | tf_op jit(solution)/shard_map/pallas_call | solution.py:115
  22.0 11.7 %shard_map.156.rows_ref = f32[32,9,128]{2,1,0:T(8,128)S(1)} custom-call(bf16[9,256,256]{2,1,0:T(8,128)(2,1)S(1)} %get-tuple-element.23.flux_ref, s32[32,128]{1,0:T(8,128)S(1)} %get-tuple-element.24.live_ref), custom_call_target="tpu_custom_call" | custom-call | tf_op jit(solution)/shard_map/pallas_call | solution.py:359
  33.7 0.0 copy-done.8
  33.7 18.1 %shard_map.157 = (f32[3,256,256]{2,1,0:T(8,128)S(1)}, f32[3,256,256]{2,1,0:T(8,128)S(1)}) custom-call(f32[32,9,128]{2,1,0:T(8,128)S(1)} %shard_map.156.rows_ref, f32[3,32,128]{2,1,0:T(8,128)S(1)} %get-tuple-element.25.area_ref, s32[32,128]{1,0:T(8,128)S(1)} %bitcast.4), custom_call_target="tpu_custom_call" | custom-call | tf_op jit(solution)/shard_map/pallas_call | solution.py:600
  51.9 0.9 %copy.20 = f32[3,256,256]{2,1,0:T(8,128)} copy(f32[3,256,256]{2,1,0:T(8,128)S(1)} %get-tuple-element.38) | data formatting | bytes 1572864
  52.8 0.9 %copy.21 = f32[3,256,256]{2,1,0:T(8,128)} copy(f32[3,256,256]{2,1,0:T(8,128)S(1)} %get-tuple-element.39) | data formatting | bytes 1572864
Async XLA Ops:
  1.4 1.0 %copy-start.2 = (f32[3,4,64,128]{3,2,1,0:T(8,128)S(1)}, f32[3,4,64,128]{3,2,1,0:T(8,128)}, u32[]{:S(2)}) copy-start(f32[3,4,64,128]{3,2,1,0:T(8,128)} %h_ref.1) | copy-start | bytes 1179652
  2.4 1.1 %copy-start.3 = (f32[3,256,256]{2,1,0:T(8,128)S(1)}, f32[3,256,256]{2,1,0:T(8,128)}, u32[]{:S(2)}) copy-start(f32[3,256,256]{2,1,0:T(8,128)} %area_any.1) | copy-start | bytes 2359300
  3.5 0.7 %copy-start.7 = (s32[1,32,128]{2,1,0:T(8,128)S(1)}, s32[1,32,128]{2,1,0:T(8,128)}, u32[]{:S(2)}) copy-start(s32[1,32,128]{2,1,0:T(8,128)} %param.20) | copy-start | bytes 49156
  4.2 0.7 %copy-start.9 = (s32[1,32,128]{2,1,0:T(8,128)S(1)}, s32[1,32,128]{2,1,0:T(8,128)}, u32[]{:S(2)}) copy-start(s32[1,32,128]{2,1,0:T(8,128)} %param.18) | copy-start | bytes 49156
  11.3 1.7 %copy-start = (f32[3,2,3,4,64,128]{5,4,3,2,1,0:T(8,128)S(1)}, f32[3,2,3,4,64,128]{5,4,3,2,1,0:T(8,128)}, u32[]{:S(2)}) copy-start(f32[3,2,3,4,64,128]{5,4,3,2,1,0:T(8,128)} %de_ref.1) | copy-start | bytes 7077892
  13.0 1.7 %copy-start.1 = (f32[3,2,3,4,64,128]{5,4,3,2,1,0:T(8,128)S(1)}, f32[3,2,3,4,64,128]{5,4,3,2,1,0:T(8,128)}, u32[]{:S(2)}) copy-start(f32[3,2,3,4,64,128]{5,4,3,2,1,0:T(8,128)} %dh_ref.1) | copy-start | bytes 7077892
  14.7 1.0 %copy-start.4 = (f32[3,4,64,128]{3,2,1,0:T(8,128)S(1)}, f32[3,4,64,128]{3,2,1,0:T(8,128)}, u32[]{:S(2)}) copy-start(f32[3,4,64,128]{3,2,1,0:T(8,128)} %e_ref.1) | copy-start | bytes 1179652
  15.7 1.0 %copy-start.5 = (f32[3,4,64,128]{3,2,1,0:T(8,128)S(1)}, f32[3,4,64,128]{3,2,1,0:T(8,128)}, u32[]{:S(2)}) copy-start(f32[3,4,64,128]{3,2,1,0:T(8,128)} %j_ref.1) | copy-start | bytes 1179652
  16.7 0.9 %copy-start.6 = (s32[4,64,128]{2,1,0:T(8,128)S(1)}, s32[4,64,128]{2,1,0:T(8,128)}, u32[]{:S(2)}) copy-start(s32[4,64,128]{2,1,0:T(8,128)} %mat_ref.1) | copy-start | bytes 393220
  17.6 0.7 %copy-start.10 = (f32[4,32]{1,0:T(4,128)S(1)}, f32[4,32]{1,0:T(4,128)}, u32[]{:S(2)}) copy-start(f32[4,32]{1,0:T(4,128)} %table_ref.1) | copy-start | bytes 1540
  18.3 15.5 %copy-start.8 = (s32[1,32,128]{2,1,0:T(8,128)S(1)}, s32[1,32,128]{2,1,0:T(8,128)}, u32[]{:S(2)}) copy-start(s32[1,32,128]{2,1,0:T(8,128)} %param.20) | copy-start | bytes 49156

commit v3 on v2

--- a/solution.py
+++ b/solution.py
@@ -15,6 +15,7 @@
 TIME_STEP = 1.9e-13
 
 
+VMEM_ALL = (64 << 20) - (256 << 10)
 MESH = pl.DeviceIdType.MESH
 
 
@@ -138,7 +139,7 @@
             jax.ShapeDtypeStruct((3 * freqs, planes * rx, 2 * cy), jnp.bfloat16),
         ],
         scratch_shapes=[pltpu.VMEM((8, cy), jnp.float32)],
-        compiler_params=pltpu.CompilerParams(vmem_limit_bytes=40 << 20),
+        compiler_params=pltpu.CompilerParams(vmem_limit_bytes=VMEM_ALL),
         cost_estimate=pl.CostEstimate(flops=10 * dft_e.size, bytes_accessed=14 << 20, transcendentals=0),
     )(h, e, j, material, table, rows, cols, dft_e, dft_h)
 
@@ -157,7 +158,7 @@
 def area_kernel(
     h_any, area_any, patch_ref, skin_ref, counts_ref,
     out_ref, live_ref, rows_ref, cols_ref,
-    h_s, area_s, split_s, row_edge, col_edge, load_sem, send_sem, recv_sem,
+    h_s, area_s, split_s, row_edge, col_edge, counts_s, limit_s, load_sem, send_sem, recv_sem,
 ):
     comps, pu, pv = area_s.shape
     blocks, cap = patch_ref.shape
@@ -210,7 +211,10 @@
         high, low = split_two(area_s[c])
         split_s[c, :, 0:pv] = high
         split_s[c, :, pv : 2 * pv] = low
-    slots = lax.broadcasted_iota(jnp.int32, (1, cap), 1)
+    slots = lax.broadcasted_iota(jnp.int32, (1, cap), 1).astype(jnp.float32)
+    counts_s[...] = jnp.zeros_like(counts_s)
+    counts_s[0:1, 0:blocks] = counts_ref[...].astype(jnp.float32)
+    limit_s[...] = jnp.broadcast_to(counts_s[0:1, :], limit_s.shape[::-1]).T
 
     def one_group(t, carry):
         for q in range(4):
@@ -226,7 +230,7 @@
                 for i in range(2):
                     out_ref[c, pl.ds(first + i, 1), :] = value[:, i * cap : (i + 1) * cap]
         here = pl.ds(pl.multiple_of(8 * t, 8), 8)
-        live_ref[here, :] = jnp.where(slots < counts_ref[here, :], skin_ref[here, :], -1)
+        live_ref[here, :] = jnp.where(slots < limit_s[here, :], skin_ref[here, :], -1)
         return carry
 
     lax.fori_loop(0, blocks // 8, one_group, 0)
@@ -246,6 +250,7 @@
     blocks, cap = patch.shape
     _, planes, rx, cy = h.shape
     edge = (2 * planes, cy)
+    lanes = -(-blocks // 128) * 128
     return pl.pallas_call(
         area_kernel,
         in_specs=[pl.BlockSpec(memory_space=pl.ANY)] * 2 + [vmem] * 3,
@@ -262,12 +267,14 @@
             pltpu.VMEM((area.shape[0], area.shape[1], 2 * area.shape[2]), jnp.bfloat16),
             pltpu.VMEM(edge, jnp.float32),
             pltpu.VMEM(edge, jnp.float32),
+            pltpu.VMEM((8, lanes), jnp.float32),
+            pltpu.VMEM((lanes, cap), jnp.float32),
             pltpu.SemaphoreType.DMA((2,)),
             pltpu.SemaphoreType.DMA((2,)),
             pltpu.SemaphoreType.DMA((2,)),
         ],
         compiler_params=pltpu.CompilerParams(
-            vmem_limit_bytes=40 << 20, collective_id=0, has_side_effects=True
+            vmem_limit_bytes=VMEM_ALL, collective_id=0, has_side_effects=True
         ),
     )(h, area, patch, skin, counts)
 
@@ -294,62 +301,43 @@
     me = lax.axis_index("gy") * n_gx + lax.axis_index("gx")
     groups = blocks // 8
     barrier = pltpu.get_barrier_semaphore()
-
-    def greet(k, carry):
-        d = (me + k) % blocks
-        signal(barrier, (d // n_gx, d % n_gx))
-        return carry
-
-    lax.fori_loop(1, blocks, greet, 0)
-
-    def gather_group(step):
-        group = (me // 8 + step) % groups
+    coords = lambda d: (d // n_gx, d % n_gx)
+    for k in range(1, blocks):
+        signal(barrier, coords((me + k) % blocks))
+
+    def gather_group(group):
         for q in range(4):
             picked = flux_pair(flux_ref, live_ref, group * 4 + q)
             for r, value in enumerate(picked):
                 for i in range(2):
                     pack_s[group * 8 + 2 * q + i, r : r + 1, :] = value[:, i * cap : (i + 1) * cap]
-        return group
 
     def copy_to(d):
-        return remote(
-            pack_s.at[d], out_ref.at[me], send_sem.at[d], recv_sem.at[me],
-            (d // n_gx, d % n_gx),
-        )
-
-    def send_group(group):
-        def send_one(i, carry):
-            d = group * 8 + i
-
-            @pl.when(d != me)
-            def _():
-                copy_to(d).start()
-
-            return carry
-
-        lax.fori_loop(0, 8, send_one, 0)
-
-    own = gather_group(0)
+        return remote(pack_s.at[d], out_ref.at[me], send_sem.at[d], recv_sem.at[me], coords(d))
+
+    mine = me // 8
+    gather_group(mine)
     out_ref[me] = pack_s[me]
     pl.semaphore_wait(barrier, blocks - 1)
-    send_group(own)
+    for k in range(1, 8):
+        copy_to(mine * 8 + (me + k) % 8).start()
+    gather_group((mine + 1) % groups)
 
     def one_step(step, carry):
-        send_group(gather_group(step))
+        ready = (mine + step - 1) % groups
+        for i in range(8):
+            copy_to(ready * 8 + i).start()
+        gather_group((mine + step) % groups)
         return carry
 
-    lax.fori_loop(1, groups, one_step, 0)
-
-    def finish(k, carry):
+    lax.fori_loop(2, groups, one_step, 0)
+    last = (mine + groups - 1) % groups
+    for i in range(8):
+        copy_to(last * 8 + i).start()
+    for k in range(1, blocks):
         d = (me + k) % blocks
         copy_to(d).wait_send()
-        remote(
-            pack_s.at[d], out_ref.at[d], send_sem.at[d], recv_sem.at[d],
-            (d // n_gx, d % n_gx),
-        ).wait_recv()
-        return carry
-
-    lax.fori_loop(1, blocks, finish, 0)
+        remote(pack_s.at[d], out_ref.at[d], send_sem.at[d], recv_sem.at[d], coords(d)).wait_recv()
 
 
 def exchange_flux(flux, live):
@@ -627,7 +615,7 @@
     blocks, cap = skin_cell.shape[1:]
     patch = patch_slot.reshape(blocks, cap)
     area_rows, live, rows_below, cols_left = gather_area(
-        h_field, area, patch, skin_cell.reshape(blocks, cap), counts.reshape(blocks, 1)
+        h_field, area, patch, skin_cell.reshape(blocks, cap), counts
     )
     e_next, j_next, dft_e_next, dft_h_next, flux = update_fields(
         h_field, e_field, j_field, material, material_table, rows_below, cols_left, dft_e, dft_h

time: 54.2 us -> 46.9 us (0.87)
  local copies, waits for them, and re-layouts: 13 us -> 3.04 us
  Pallas kernels: 40 us -> 42.9 us
    unnamed x24 -> x10, local copies, waits for them, and re-layouts: 12.2 us -> 3.04 us
    pallas_call x1, Pallas kernels: 3.71 us -> 5.7 us  [update_fields(): pl.pallas_call(field_kernel, grid=(planes // per,), in_specs=[pl.BlockSpe...]
    pallas_call x1, Pallas kernels: 6.4 us -> 7.71 us  [gather_area(): pl.pallas_call(area_kernel, in_specs=[pl.BlockSpec(memory_space=pl.ANY)]...]
    reshape x1 -> x0, local copies, waits for them, and re-layouts: 0.74 us -> none  [shards(): counts.reshape(blocks, 1)]
    pallas_call x1, Pallas kernels: 11.7 us -> 11.1 us  [exchange_flux(): pl.pallas_call(flux_kernel, in_specs=[vmem, vmem], out_specs=vmem, out_sh...]
where the time goes in v3:
time: 46.9 us; the launch traced here: 46.7 us
  Pallas kernels  42.9 us (91%)
  local copies, waits for them, and re-layouts  3.04 us (6%)
  between operations  0.71 us (2%)
    pallas_call x1, Pallas kernels, surface(): pl.pallas_call(band_kernel, in_specs=[vmem] * 3, out_specs=[vmem] * 2, ou...  18.4 us
    pallas_call x1, Pallas kernels, exchange_flux(): pl.pallas_call(flux_kernel, in_specs=[vmem, vmem], out_specs=vmem, out_sh...  11.1 us
    pallas_call x1, Pallas kernels, gather_area(): pl.pallas_call(area_kernel, in_specs=[pl.BlockSpec(memory_space=pl.ANY)]...  7.71 us
    pallas_call x1, Pallas kernels, update_fields(): pl.pallas_call(field_kernel, grid=(planes // per,), in_specs=[pl.BlockSpe...  5.7 us
    unnamed x10, local copies, waits for them, and re-layouts  3.04 us

profile of v3, /device:TPU:21, one launch (start us, length us, event | category | flops | bytes accessed | tf_op | source)
XLA Modules:
  0.0 46.7 jit_solution(557266627970190831)
XLA Ops:
  0.6 7.7 %shard_map.154 = (f32[3,32,128]{2,1,0:T(8,128)}, s32[32,128]{1,0:T(8,128)}, f32[8,128]{1,0:T(8,128)}, f32[8,128]{1,0:T(8,128)}) custom-call(f32[3,4,64,128]{3,2,1,0:T(8,128)} %h_ref.1, f32[3,256,256]{2,1,0:T(8,128)} %area_any.1, s32[32,128]{1,0:T(8,128)} %bitcast.2, s32[32,128]{1,0:T(8,128)} %bitcast.4, s32[1,32]{1,0:T(1,128)} %counts_ref.1), custom_call_target="tpu_custom_call" | custom-call | tf_op jit(solution)/shard_map/pallas_call | solution.py:254
  8.4 0.0 copy-start.3
  8.4 0.0 copy-start.1
  8.4 0.0 copy-start.2
  8.4 5.7 %shard_map.155 = (f32[3,4,64,128]{3,2,1,0:T(8,128)}, f32[3,4,64,128]{3,2,1,0:T(8,128)}, f32[3,2,3,4,64,128]{5,4,3,2,1,0:T(8,128)}, f32[3,2,3,4,64,128]{5,4,3,2,1,0:T(8,128)}, bf16[9,256,256]{2,1,0:T(8,128)(2,1)}) custom-call(f32[3,4,64,128]{3,2,1,0:T(8,128)} %h_ref.1, f32[3,4,64,128]{3,2,1,0:T(8,128)} %e_ref.1, f32[3,4,64,128]{3,2,1,0:T(8,128)} %j_ref.1, ...), custom_call_target="tpu_custom_call" | custom-call | flops 5898240 | bytes 14680064 | tf_op jit(solution)/shard_map/pallas_call | solution.py:116
  14.1 0.0 copy-done.3
  14.1 0.0 copy-start
  14.1 1.3 %copy-done = bf16[9,256,256]{2,1,0:T(8,128)(2,1)S(1)} copy-done((bf16[9,256,256]{2,1,0:T(8,128)(2,1)S(1)}, bf16[9,256,256]{2,1,0:T(8,128)(2,1)}, u32[]{:S(2)}) %copy-start) | copy-done | bytes 1179672
  15.4 11.1 %shard_map.156.rows_ref = f32[32,9,128]{2,1,0:T(8,128)S(1)} custom-call(bf16[9,256,256]{2,1,0:T(8,128)(2,1)S(1)} %copy-done, s32[32,128]{1,0:T(8,128)S(1)} %copy-done.3), custom_call_target="tpu_custom_call" | custom-call | tf_op jit(solution)/shard_map/pallas_call | solution.py:347
  26.4 0.0 copy-done.1
  26.4 0.0 copy-done.2
  26.5 18.4 %shard_map.157 = (f32[3,256,256]{2,1,0:T(8,128)S(1)}, f32[3,256,256]{2,1,0:T(8,128)S(1)}) custom-call(f32[32,9,128]{2,1,0:T(8,128)S(1)} %shard_map.156.rows_ref, f32[3,32,128]{2,1,0:T(8,128)S(1)} %copy-done.2, s32[32,128]{1,0:T(8,128)S(1)} %bitcast.3), custom_call_target="tpu_custom_call" | custom-call | tf_op jit(solution)/shard_map/pallas_call | solution.py:588
  44.9 0.9 %copy.19 = f32[3,256,256]{2,1,0:T(8,128)} copy(f32[3,256,256]{2,1,0:T(8,128)S(1)} %get-tuple-element.38) | data formatting | bytes 1572864
  45.8 0.9 %copy.20 = f32[3,256,256]{2,1,0:T(8,128)} copy(f32[3,256,256]{2,1,0:T(8,128)S(1)} %get-tuple-element.39) | data formatting | bytes 1572864
Async XLA Ops:
  8.4 5.7 %copy-start.3 = (s32[32,128]{1,0:T(8,128)S(1)}, s32[32,128]{1,0:T(8,128)}, u32[]{:S(2)}) copy-start(s32[32,128]{1,0:T(8,128)} %get-tuple-element.24.live_ref) | copy-start | bytes 49156
  8.4 18.1 %copy-start.1 = (s32[1,32,128]{2,1,0:T(8,128)S(1)}, s32[1,32,128]{2,1,0:T(8,128)}, u32[]{:S(2)}) copy-start(s32[1,32,128]{2,1,0:T(8,128)} %param.20) | copy-start | bytes 49156
  8.4 18.1 %copy-start.2 = (f32[3,32,128]{2,1,0:T(8,128)S(1)}, f32[3,32,128]{2,1,0:T(8,128)}, u32[]{:S(2)}) copy-start(f32[3,32,128]{2,1,0:T(8,128)} %get-tuple-element.25.area_ref) | copy-start | bytes 147460
  14.1 1.3 %copy-start = (bf16[9,256,256]{2,1,0:T(8,128)(2,1)S(1)}, bf16[9,256,256]{2,1,0:T(8,128)(2,1)}, u32[]{:S(2)}) copy-start(bf16[9,256,256]{2,1,0:T(8,128)(2,1)} %get-tuple-element.23.flux_ref) | copy-start | bytes 3538948
